TPU v7x, 512 devices: a whole 4x8x8 slice. The times are simulated.
512 devices in a mesh: py: 16 (over z_lo, x, core), pz: 32 (over y, z_hi).
Axes of the slice: x: 4, y: 8, z: 8 (z_hi: 4, z_lo: 2; z = z_hi * 2 + z_lo), core: 2. Of those that a mesh axis runs over, the one named last changes fastest.
Arguments:
- cotangent: float32 [8, 524288], P(None, ('py', 'pz')), may hold values from -6 to 6
- spline_weights: float32 [64, 524288], P(None, ('py', 'pz')), may hold values from 0 to 0.25
- base_cells: int32 [3, 524288], P(None, ('py', 'pz')), may hold values from 0 to 127, as said below
- spectral_filter: float32 [8, 128, 128, 128], P(None, 'pz', 'py'), may hold values from -3 to 6, as said below
Outputs:
- feature_grad: float32 [8, 524288], P(None, ('py', 'pz'))
Inputs may be any that keep to these rules, and one draw needn't show every extreme that they name: Atom a lies in the block of the device that holds it: base_cells[0, a] // 8 * 32 + base_cells[1, a] // 4 equals a // 1024, with 32 the devices along pz. spectral_filter[c, kz, ky, kx] equals spectral_filter[c, -kz, -ky, -kx], indices taken modulo 128.
All inputs are finite; a program needn't handle non-finite values.
Results may differ from a plain program's by a relative error of at most 0.00005.
Values sent between devices are 32-bit elements; how exact they have to be, the bound alone decides.
No kernel may reach another device: no remote copies, remote signals or barrier semaphores. Data moves between devices by JAX's collectives and lax.ppermute only.
A program may use at most 128 MiB of HBM per device.

v0:
```python
import math

import jax
import jax.numpy as jnp
from jax import lax
from jax.sharding import PartitionSpec as P

MESH = 128


exact_mode = lax.Precision.HIGHEST


def passed_along(block, axis, distance):
    devices = range(lax.axis_size(axis))
    route = [((i - distance) % len(devices), i) for i in devices]
    return lax.ppermute(block, axis, route)


def trig_tables(length, columns):
    product = jnp.arange(length, dtype=jnp.int32)[:, None] * columns[None, :] % length
    angle = product.astype(jnp.float32) * (2.0 * math.pi / length)
    return (jnp.cos(angle), jnp.sin(angle))


def stencil_cells(local_x, local_y, base_z, step_x, ext_y):
    offsets = jnp.arange(16, dtype=jnp.int32)
    shift_y = offsets // 4
    shift_z = offsets % 4
    row_part = (local_x[None, :] + step_x) * ext_y + local_y[None, :] + shift_y[:, None]
    return row_part * MESH + (base_z[None, :] + shift_z[:, None]) % MESH


def on_device(cotangent, spline_weights, base_cells, spectral_filter):
    channels, atom_count = cotangent.shape
    rows_dev = lax.axis_size("py")
    cols_dev = lax.axis_size("pz")
    block_x = MESH // rows_dev
    block_y = MESH // cols_dev
    ext_x = block_x + 3
    ext_y = block_y + 3
    row_id = lax.axis_index("py")
    col_id = lax.axis_index("pz")
    local_x = base_cells[0] - row_id * block_x
    local_y = base_cells[1] - col_id * block_y
    base_z = base_cells[2]
    extended = jnp.zeros((channels, ext_x * ext_y * MESH), jnp.float32)
    for step_x in range(4):
        cells = stencil_cells(local_x, local_y, base_z, step_x, ext_y)
        values = cotangent[:, None, :] * spline_weights[16 * step_x : 16 * step_x + 16][None]
        extended = extended.at[:, cells.reshape(-1)].add(values.reshape(channels, -1))
    extended = extended.reshape(channels, ext_x, ext_y, MESH)
    arrived = passed_along(extended[:, block_x:], "py", 1)
    core = extended[:, :block_x]
    core = jnp.concatenate([core[:, :3] + arrived, core[:, 3:]], axis=1)
    arrived = passed_along(core[:, :, block_y:], "pz", 1)
    core = core[:, :, :block_y]
    density = jnp.concatenate([core[:, :, :3] + arrived, core[:, :, 3:]], axis=2)
    kept_cols = jnp.arange(MESH, dtype=jnp.int32)
    fold_factor = jnp.ones((MESH,), jnp.float32)
    cos_z, sin_z = trig_tables(MESH, kept_cols)
    cos_full, sin_full = trig_tables(MESH, jnp.arange(MESH, dtype=jnp.int32))
    real_part = jnp.dot(density, cos_z, precision=exact_mode)
    imag_part = -jnp.dot(density, sin_z, precision=exact_mode)
    first = lax.all_to_all(real_part, "pz", split_axis=3, concat_axis=2, tiled=True)
    second = lax.all_to_all(imag_part, "pz", split_axis=3, concat_axis=2, tiled=True)
    out_real = jnp.einsum("cxyz,yk->cxzk", first, cos_full, precision=exact_mode) + jnp.einsum(
        "cxyz,yk->cxzk", second, sin_full, precision=exact_mode
    )
    out_imag = jnp.einsum("cxyz,yk->cxzk", second, cos_full, precision=exact_mode) - jnp.einsum(
        "cxyz,yk->cxzk", first, sin_full, precision=exact_mode
    )
    real_part = out_real
    imag_part = out_imag
    first = lax.all_to_all(real_part, "py", split_axis=3, concat_axis=1, tiled=True)
    second = lax.all_to_all(imag_part, "py", split_axis=3, concat_axis=1, tiled=True)
    out_real = jnp.einsum("cxzk,xq->czkq", first, cos_full, precision=exact_mode) + jnp.einsum(
        "cxzk,xq->czkq", second, sin_full, precision=exact_mode
    )
    out_imag = jnp.einsum("cxzk,xq->czkq", second, cos_full, precision=exact_mode) - jnp.einsum(
        "cxzk,xq->czkq", first, sin_full, precision=exact_mode
    )
    real_part = out_real
    imag_part = out_imag
    real_part = real_part * spectral_filter
    imag_part = imag_part * spectral_filter
    back_real = jnp.dot(real_part, cos_full, precision=exact_mode) - jnp.dot(
        imag_part, sin_full, precision=exact_mode
    )
    back_imag = jnp.dot(imag_part, cos_full, precision=exact_mode) + jnp.dot(
        real_part, sin_full, precision=exact_mode
    )
    first = lax.all_to_all(back_real, "py", split_axis=3, concat_axis=2, tiled=True)
    second = lax.all_to_all(back_imag, "py", split_axis=3, concat_axis=2, tiled=True)
    out_real = jnp.einsum("czyx,yn->czxn", first, cos_full, precision=exact_mode) - jnp.einsum(
        "czyx,yn->czxn", second, sin_full, precision=exact_mode
    )
    out_imag = jnp.einsum("czyx,yn->czxn", second, cos_full, precision=exact_mode) + jnp.einsum(
        "czyx,yn->czxn", first, sin_full, precision=exact_mode
    )
    scale = 1.0 / float(MESH) ** 3
    cos_back = cos_z.T * (fold_factor * scale)[:, None]
    sin_back = sin_z.T * (fold_factor * scale)[:, None]
    first = lax.all_to_all(out_real, "pz", split_axis=3, concat_axis=1, tiled=True)
    second = lax.all_to_all(out_imag, "pz", split_axis=3, concat_axis=1, tiled=True)
    potential = jnp.einsum("czxy,zn->cxyn", first, cos_back, precision=exact_mode) - jnp.einsum(
        "czxy,zn->cxyn", second, sin_back, precision=exact_mode
    )
    below = passed_along(potential[:, :3], "py", -1)
    widened = jnp.concatenate([potential, below], axis=1)
    beside = passed_along(widened[:, :, :3], "pz", -1)
    widened = jnp.concatenate([widened, beside], axis=2).reshape(channels, -1)
    feature_grad = jnp.zeros((channels, atom_count), jnp.float32)
    for step_x in range(4):
        cells = stencil_cells(local_x, local_y, base_z, step_x, ext_y)
        picked = widened[:, cells]
        feature_grad = feature_grad + jnp.sum(
            picked * spline_weights[16 * step_x : 16 * step_x + 16][None], axis=1
        )
    return feature_grad


def solution(mesh):
    return jax.shard_map(
        on_device,
        mesh=mesh,
        in_specs=(
            P(None, ("py", "pz")),
            P(None, ("py", "pz")),
            P(None, ("py", "pz")),
            P(None, "pz", "py", None),
        ),
        out_specs=P(None, ("py", "pz")),
        check_vma=False,
    )
```

profile of v0, /device:TPU:1, one launch (start us, length us, event | category | flops | bytes accessed | tf_op | source)
XLA Modules:
  0.0 862.3 jit_solution(14438856337820044779)
XLA Ops:
  4.0 13.8 %bitcast_multiply_fusion = (f32[8,16384]{0,1:T(8,128)}, f32[8,16384]{0,1:T(8,128)}, f32[8,16384]{0,1:T(8,128)}, f32[8,16384]{0,1:T(8,128)}) fusion(f32[16384]{0:T(1024)S(1)} %bitcast.265, f32[8,1024]{0,1:T(8,128)S(1)} %copy.42, f32[16384]{0:T(1024)S(1)} %bitcast.264, f32[16384]{0:T(1024)S(1)} %bitcast.263, f32[16384]{0:T(1024)S(1)} %bitcast.262), kind=kLoop, calls=%fused_computation.8 | loop fusion | flops 524288 | bytes 2392064 | tf_op jit(solution)/shard_map/mul | solution.py:50
  17.8 82.3 %scatter_custom_fusion = f32[8,9856]{0,1:T(8,128)} fusion(s32[16384]{0:T(1024)S(1)} %bitcast.277, f32[8,16384]{0,1:T(8,128)} %get-tuple-element.10, f32[]{:T(128)} %constant.126.clone.1), kind=kCustom, calls=%fused_computation.18 | custom fusion | flops 131072 | bytes 839684 | tf_op jit(solution)/shard_map/scatter-add | solution.py:51
  100.2 92.9 %scatter_custom_fusion.1 = f32[8,9856]{0,1:T(8,128)} fusion(f32[8,9856]{0,1:T(8,128)} %scatter_custom_fusion, s32[16384]{0:T(1024)S(1)} %bitcast.276, f32[8,16384]{0,1:T(8,128)} %get-tuple-element.9), kind=kCustom, calls=%fused_computation.16 | custom fusion | flops 131072 | bytes 8704000 | tf_op jit(solution)/shard_map/scatter-add | solution.py:51
  193.1 92.9 %scatter_custom_fusion.2 = f32[8,9856]{0,1:T(8,128)} fusion(f32[8,9856]{0,1:T(8,128)} %scatter_custom_fusion.1, s32[16384]{0:T(1024)S(1)} %bitcast.275, f32[8,16384]{0,1:T(8,128)} %get-tuple-element.8), kind=kCustom, calls=%fused_computation.14 | custom fusion | flops 131072 | bytes 8704000 | tf_op jit(solution)/shard_map/scatter-add | solution.py:51
  286.0 92.9 %scatter_custom_fusion.3 = f32[8,9856]{0,1:T(8,128)} fusion(f32[8,9856]{0,1:T(8,128)} %scatter_custom_fusion.2, s32[16384]{0:T(1024)S(1)} %bitcast.278, f32[8,16384]{0,1:T(8,128)} %get-tuple-element.7), kind=kCustom, calls=%fused_computation.12 | custom fusion | flops 131072 | bytes 8704000 | tf_op jit(solution)/shard_map/scatter-add | solution.py:51
  378.9 3.5 copy.43
  382.4 4.5 collective-permute-start
  387.0 5.0 collective-permute-done
  392.1 3.0 collective-permute-start.1
  395.2 10.3 %collective-permute-done.1 = f32[8,8,3,128]{3,1,2,0:T(8,128)S(1)} collective-permute-done((f32[8,8,3,128]{3,1,2,0:T(8,128)S(1)}, f32[8,8,3,128]{3,1,2,0:T(8,128)S(1)}, u32[]{:S(2)}, u32[]{:S(2)}) %collective-permute-start.1) | collective-permute-done | bytes 98336 | tf_op jit(solution)/shard_map/ppermute | solution.py:17
  406.0 1.5 copy.47
  407.5 3.1 reshape.879
  410.6 6.6 all-to-all-start
  419.3 3.1 reshape.877
  422.3 6.2 all-to-all-done
  428.5 5.6 all-to-all-start.1
  435.6 2.5 reshape.880
  440.2 5.2 all-to-all-done.1
  446.4 2.5 reshape.878
  452.5 3.1 reshape.883
  455.6 10.7 %all-to-all-start.2 = ((f32[16,1,2048]{2,1,0:T(1,128)}), f32[16,1,2048]{2,1,0:T(1,128)S(1)}, u32[]{:S(2)}, u32[]{:S(2)}) async-start(f32[16,1,2048]{2,1,0:T(1,128)} %reshape.883), calls=%async_computation.2 | async-start | bytes 262144 | tf_op jit(solution)/shard_map/all_to_all | solution.py:75
  467.3 1.5 copy.60
  468.8 3.1 reshape.881
  472.4 5.7 all-to-all-start.3
  479.3 2.5 reshape.884
  481.8 2.6 copy.125
  484.3 2.6 all_to_all.115
  488.5 2.5 reshape.882
  491.0 2.6 copy.124
  493.5 2.6 all_to_all.119
  498.8 1.7 copy.63
  500.5 3.1 reshape.887
  503.6 5.7 all-to-all-start.4
  511.8 3.1 reshape.885
  515.4 5.2 all-to-all-start.5
  521.7 2.5 reshape.888
  524.1 2.6 copy.123
  526.7 2.6 all_to_all.123
  530.9 2.5 reshape.886
  533.3 2.6 copy.122
  535.9 2.6 all_to_all.127
  540.6 3.1 reshape.891
  543.7 5.7 all-to-all-start.6
  551.9 3.1 reshape.889
  555.0 5.7 all-to-all-done.6
  560.7 6.2 all-to-all-start.7
  567.8 2.5 reshape.892
  570.7 7.5 all-to-all-done.7
  579.2 3.9 reshape.890
  583.0 1.7 copy.74
  585.0 4.1 fusion.9
  589.1 4.1 fusion.15
  593.1 3.9 collective-permute-start.2
  597.0 3.4 collective-permute-done.2
  600.5 3.3 collective-permute-start.3
  603.8 10.3 %collective-permute-done.3 = f32[8,11,3,128]{3,1,2,0:T(8,128)S(1)} collective-permute-done((f32[8,11,3,128]{3,1,2,0:T(8,128)S(1)}, f32[8,11,3,128]{3,1,2,0:T(8,128)S(1)}, u32[]{:S(2)}, u32[]{:S(2)}) %collective-permute-start.3) | collective-permute-done | bytes 135200 | tf_op jit(solution)/shard_map/ppermute | solution.py:17
  614.2 3.6 copy.78
  617.8 56.8 %gather_fusion = f32[16384,8]{1,0:T(8,128)} fusion(f32[8,9856]{0,1:T(8,128)} %copy.78, s32[16384]{0:T(1024)S(1)} %broadcast_clamp_fusion.3), kind=kCustom, calls=%fused_computation | custom fusion | bytes 1114112 | tf_op jit(solution)/shard_map/gather | solution.py:116
  674.6 56.8 %gather_fusion.1 = f32[16384,8]{1,0:T(8,128)} fusion(f32[8,9856]{0,1:T(8,128)} %copy.78, s32[16384]{0:T(1024)S(1)} %broadcast_clamp_fusion.2), kind=kCustom, calls=%fused_computation.1 | custom fusion | bytes 1114112 | tf_op jit(solution)/shard_map/gather | solution.py:116
  731.4 56.8 %gather_fusion.2 = f32[16384,8]{1,0:T(8,128)} fusion(f32[8,9856]{0,1:T(8,128)} %copy.78, s32[16384]{0:T(1024)S(1)} %broadcast_clamp_fusion.1), kind=kCustom, calls=%fused_computation.2 | custom fusion | bytes 1114112 | tf_op jit(solution)/shard_map/gather | solution.py:116
  788.2 56.8 %gather_fusion.3 = f32[16384,8]{1,0:T(8,128)} fusion(f32[8,9856]{0,1:T(8,128)} %copy.78, s32[16384]{0:T(1024)S(1)} %broadcast_clamp_fusion), kind=kCustom, calls=%fused_computation.3 | custom fusion | bytes 1114112 | tf_op jit(solution)/shard_map/gather | solution.py:116
  845.1 9.3 %multiply_reduce_fusion.2 = (f32[1024,8]{1,0:T(8,128)S(1)}, f32[1024,8]{1,0:T(8,128)S(1)}) fusion(f32[16,1024,8]{2,1,0:T(8,128)} %bitcast.230, f32[16,1024]{1,0:T(8,128)S(1)} %get-tuple-element.13, f32[16,1024,8]{2,1,0:T(8,128)} %bitcast.229, f32[16,1024]{1,0:T(8,128)S(1)} %get-tuple-element.18), kind=kLoop, calls=%fused_computation.22 | loop fusion | flops 507904 | bytes 1245184 | tf_op jit(solution)/shard_map/reduce_sum | solution.py:117
  854.4 1.6 copy-done
  856.0 5.0 multiply_reduce_fusion
  (94 shorter events, 35.1 us)
Async XLA Ops:
  382.4 9.6 %collective-permute-start = (f32[8,3,7,128]{3,1,2,0:T(4,128)S(1)}, f32[8,3,7,128]{3,1,2,0:T(4,128)S(1)}, u32[]{:S(2)}, u32[]{:S(2)}) collective-permute-start(f32[8,3,7,128]{3,1,2,0:T(4,128)S(1)} %copy.96), channel_id=1, source_target_pairs={{480,0},{0,32},{32,64},{64,96},{96,128},{128,160},{160,192},{192,2... | collective-permute-start | bytes 258056 | tf_op jit(solution)/shard_map/ppermute | solution.py:17
  392.1 13.3 %collective-permute-start.1 = (f32[8,8,3,128]{3,1,2,0:T(8,128)S(1)}, f32[8,8,3,128]{3,1,2,0:T(8,128)S(1)}, u32[]{:S(2)}, u32[]{:S(2)}) collective-permute-start(f32[8,8,3,128]{3,1,2,0:T(8,128)S(1)} %fusion.19), channel_id=1, source_target_pairs={{31,0},{0,1},{1,2},{2,3},{3,4},{4,5},{5,6},{6,7},{7,8},{8,9},{9,10... | collective-permute-start | bytes 294920 | tf_op jit(solution)/shard_map/ppermute | solution.py:17
  410.6 17.9 %all-to-all-start = ((f32[32,1,1024]{2,1,0:T(1,128)}), f32[32,1,1024]{2,1,0:T(1,128)S(1)}, u32[]{:S(2)}, u32[]{:S(2)}) async-start(f32[32,1,1024]{2,1,0:T(1,128)} %reshape.879), calls=%async_computation | async-start | bytes 262144 | tf_op jit(solution)/shard_map/all_to_all | solution.py:65
  428.5 16.9 %all-to-all-start.1 = ((f32[32,1,1024]{2,1,0:T(1,128)}), f32[32,1,1024]{2,1,0:T(1,128)S(1)}, u32[]{:S(2)}, u32[]{:S(2)}) async-start(f32[32,1,1024]{2,1,0:T(1,128)} %reshape.877), calls=%async_computation.1 | async-start | bytes 262144 | tf_op jit(solution)/shard_map/all_to_all | solution.py:66
  455.6 16.8 %all-to-all-start.2 = ((f32[16,1,2048]{2,1,0:T(1,128)}), f32[16,1,2048]{2,1,0:T(1,128)S(1)}, u32[]{:S(2)}, u32[]{:S(2)}) async-start(f32[16,1,2048]{2,1,0:T(1,128)} %reshape.883), calls=%async_computation.2 | async-start | bytes 262144 | tf_op jit(solution)/shard_map/all_to_all | solution.py:75
  472.4 15.1 %all-to-all-start.3 = ((f32[16,1,2048]{2,1,0:T(1,128)}), f32[16,1,2048]{2,1,0:T(1,128)S(1)}, u32[]{:S(2)}, u32[]{:S(2)}) async-start(f32[16,1,2048]{2,1,0:T(1,128)} %reshape.881), calls=%async_computation.3 | async-start | bytes 262144 | tf_op jit(solution)/shard_map/all_to_all | solution.py:76
  487.0 9.7 %copy-start.1 = (f32[8,4,8,128]{3,2,1,0:T(8,128)S(1)}, f32[8,4,8,128]{3,2,1,0:T(8,128)}, u32[]{:S(2)}) copy-start(f32[8,4,8,128]{3,2,1,0:T(8,128)} %param.7) | copy-start | bytes 393220
  503.6 11.9 %all-to-all-start.4 = ((f32[16,1,2048]{2,1,0:T(1,128)}), f32[16,1,2048]{2,1,0:T(1,128)S(1)}, u32[]{:S(2)}, u32[]{:S(2)}) async-start(f32[16,1,2048]{2,1,0:T(1,128)} %reshape.887), calls=%async_computation.4 | async-start | bytes 262144 | tf_op jit(solution)/shard_map/all_to_all | solution.py:93
  515.4 14.5 %all-to-all-start.5 = ((f32[16,1,2048]{2,1,0:T(1,128)}), f32[16,1,2048]{2,1,0:T(1,128)S(1)}, u32[]{:S(2)}, u32[]{:S(2)}) async-start(f32[16,1,2048]{2,1,0:T(1,128)} %reshape.885), calls=%async_computation.5 | async-start | bytes 262144 | tf_op jit(solution)/shard_map/all_to_all | solution.py:94
  543.7 17.0 %all-to-all-start.6 = ((f32[32,1,1024]{2,1,0:T(1,128)}), f32[32,1,1024]{2,1,0:T(1,128)S(1)}, u32[]{:S(2)}, u32[]{:S(2)}) async-start(f32[32,1,1024]{2,1,0:T(1,128)} %reshape.891), calls=%async_computation.6 | async-start | bytes 262144 | tf_op jit(solution)/shard_map/all_to_all | solution.py:104
  560.7 17.5 %all-to-all-start.7 = ((f32[32,1,1024]{2,1,0:T(1,128)}), f32[32,1,1024]{2,1,0:T(1,128)S(1)}, u32[]{:S(2)}, u32[]{:S(2)}) async-start(f32[32,1,1024]{2,1,0:T(1,128)} %reshape.889), calls=%async_computation.7 | async-start | bytes 262144 | tf_op jit(solution)/shard_map/all_to_all | solution.py:105
  593.1 7.3 collective-permute-start.2
  600.5 13.6 %collective-permute-start.3 = (f32[8,11,3,128]{3,1,2,0:T(8,128)S(1)}, f32[8,11,3,128]{3,1,2,0:T(8,128)S(1)}, u32[]{:S(2)}, u32[]{:S(2)}) collective-permute-start(f32[8,11,3,128]{3,1,2,0:T(8,128)S(1)} %pad_maximum_fusion.1), channel_id=1, source_target_pairs={{1,0},{2,1},{3,2},{4,3},{5,4},{6,5},{7,6},{8,7},{9,8},{10,9},{11,1... | collective-permute-start | bytes 405512 | tf_op jit(solution)/shard_map/ppermute | solution.py:17
  845.1 9.3 %slice-start = ((s8[8388608]{0:T(1024)(128)(4,1)}), s8[4194304]{0:T(1024)(128)(4,1)S(1)}, s32[]{:S(2)}) async-start(s8[8388608]{0:T(1024)(128)(4,1)} %bitcast.225), calls=%async_computation.8 | async-start | bytes 8388608
  845.1 9.3 %slice-start.1 = ((s8[8388608]{0:T(1024)(128)(4,1)}), s8[4194304]{0:T(1024)(128)(4,1)S(1)}, s32[]{:S(2)}) async-start(s8[8388608]{0:T(1024)(128)(4,1)} %bitcast.225), calls=%async_computation.9 | async-start | bytes 8388608
  845.1 10.9 %copy-start = (f32[16384,8]{1,0:T(8,128)S(1)}, f32[16384,8]{1,0:T(8,128)}, u32[]{:S(2)}) copy-start(f32[16384,8]{1,0:T(8,128)} %gather_fusion.3) | copy-start | bytes 1572868
where the time goes:
time: 872 us; the launch traced here: 862 us
  other arithmetic  399 us (46%)
  local copies, waits for them, and re-layouts  324 us (37%)
  starting transfers between devices  66.1 us (8%)
  waiting for transfers between devices  54.6 us (6%)
  matrix products  17.3 us (2%)
    scatter-add x4, other arithmetic, on_device(): extended.at[:, cells.reshape(-1)].add(values.reshape(channels, -1))  361 us
    gather x4, local copies, waits for them, and re-layouts, on_device(): picked = widened[:, cells]  227 us
    unnamed x40, local copies, waits for them, and re-layouts  48.8 us
    ppermute x4, waiting for transfers between devices, passed_along(): return lax.ppermute(block, axis, route)  28.9 us
  transfers between devices with their start and end apart: 12, of which 10 were waited for; matrix products, arithmetic and copies ran while one was open for 5% of the time, Pallas kernels for 0%

commit v1 on v0

v1 whole, which is shorter than its diff:
```python
import math

import jax
import jax.numpy as jnp
import ml_dtypes
import numpy as np
from jax import lax
from jax.experimental import pallas as pl
from jax.experimental.pallas import tpu as pltpu
from jax.sharding import PartitionSpec as P

MESH = 128
CH = 8
PY = 16
PZ = 32
BX = MESH // PY
BY = MESH // PZ
EX = BX + 3
ROWS = EX * 8
LANES = 128
TILE = 128

F32 = jnp.float32
BF16 = jnp.bfloat16


def halves(table):
    high = table.astype(ml_dtypes.bfloat16)
    low = (table - high.astype(np.float64)).astype(ml_dtypes.bfloat16)
    return high, low


def turn(numerator, denominator):
    angle = 2.0 * math.pi * (numerator % denominator) / denominator
    return np.cos(angle) + 1j * np.sin(angle)


def z_tables():
    z = np.arange(MESH)
    forth = np.zeros((2, PZ, 2, MESH))
    back = np.zeros((2, PZ, 2, MESH))
    scale = 1.0 / float(MESH) ** 3
    for s in range(2):
        for q in range(PZ):
            kz = 4 * q + s + (1 if q >= PZ // 2 else 0)
            wave = turn(kz * z, MESH)
            forth[s, q, 0] = wave.real
            forth[s, q, 1] = -wave.imag
            back[s, q, 0] = 2.0 * scale * wave.real
            back[s, q, 1] = -2.0 * scale * wave.imag
    sign = 1.0 - 2.0 * (z % 2)
    forth[0, 0, 0] = 1.0
    forth[0, 0, 1] = sign
    back[0, 0, 0] = scale
    back[0, 0, 1] = scale * sign
    return forth.reshape(128, MESH), back.reshape(128, MESH)


def plane_tables():
    k0 = np.arange(PZ)
    wave = turn(-np.outer(k0, np.arange(PZ)), PZ)
    first = np.zeros((2, PZ, PZ, 2))
    first[0, :, :, 0] = wave.real
    first[0, :, :, 1] = -wave.imag
    first[1, :, :, 0] = wave.imag
    first[1, :, :, 1] = wave.real
    first = np.kron(np.eye(4), first.reshape(64, 64))
    xl = np.zeros(LANES, np.int64)
    yl = np.zeros(LANES, np.int64)
    used = np.zeros(LANES)
    for x in range(EX):
        for y in range(BY + 3):
            xl[8 * x + y] = x
            yl[8 * x + y] = y
            used[8 * x + y] = 1.0
    kx0 = np.repeat(np.arange(PY), PZ)
    ky0 = np.tile(np.arange(PZ), PY)
    twist = turn(-(kx0[:, None] * xl[None] + ky0[:, None] * yl[None]), MESH) * used
    m = np.repeat(np.arange(8), 4)
    n = np.tile(np.arange(4), 8)
    fine = turn(-(4 * m[None] * xl[:, None] + 8 * n[None] * yl[:, None]), 32) * used[:, None]
    second = np.zeros((2, LANES, 2, 2, 32))
    for ab in range(2):
        second[0, :, ab, 0] = fine.real
        second[1, :, ab, 0] = -fine.imag
        second[0, :, ab, 1] = fine.imag
        second[1, :, ab, 1] = fine.real
    third = np.zeros((2, 2, 32, 2, 2, LANES))
    for ab in range(2):
        third[ab, 0, :, ab, 0] = fine.real.T
        third[ab, 1, :, ab, 0] = fine.imag.T
        third[ab, 0, :, ab, 1] = -fine.imag.T
        third[ab, 1, :, ab, 1] = fine.real.T
    last = np.zeros((PZ, 2, 2, 2, PZ))
    last[:, 0, 0, 0] = wave.real.T
    last[:, 0, 0, 1] = wave.imag.T
    last[:, 1, 1, 0] = -wave.imag.T
    last[:, 1, 1, 1] = wave.real.T
    last = np.kron(np.eye(2), last.reshape(64, 128))
    twist = np.stack([twist.real, twist.imag]).astype(np.float32)
    return first, twist, second.reshape(256, 128), third.reshape(128, 512), last


def split(value):
    high = value.astype(BF16)
    return high, (value - high.astype(F32)).astype(BF16)


def mm(a, b, dims=((1,), (0,))):
    return lax.dot_general(a, b, (dims, ((), ())), preferred_element_type=F32)


def fft4(x, sign):
    (ar, ai), (br, bi), (cr, ci), (dr, di) = x
    sr, si, tr, ti = ar + cr, ai + ci, ar - cr, ai - ci
    ur, ui, vr, vi = br + dr, bi + di, br - dr, bi - di
    if sign < 0:
        return [(sr + ur, si + ui), (tr + vi, ti - vr), (sr - ur, si - ui), (tr - vi, ti + vr)]
    return [(sr + ur, si + ui), (tr - vi, ti + vr), (sr - ur, si - ui), (tr + vi, ti - vr)]


def times(value, k, sign):
    re, im = value
    k %= 16
    if k == 0:
        return value
    if k == 4:
        return (-sign * im, sign * re)
    c, s = math.cos(2.0 * math.pi * k / 16), sign * math.sin(2.0 * math.pi * k / 16)
    if k in (2, 6):
        h = math.sqrt(0.5)
        if k == 2:
            return ((re - sign * im) * h, (im + sign * re) * h)
        return ((re + sign * im) * -h, (sign * re - im) * h)
    return (re * c - im * s, im * c + re * s)


def fft16(x, sign):
    inner = [fft4([x[4 * a + b] for a in range(4)], sign) for b in range(4)]
    out = [None] * 16
    for k in range(4):
        column = fft4([times(inner[b][k], b * k, sign) for b in range(4)], sign)
        for a in range(4):
            out[k + 4 * a] = column[a]
    return out


def atom_weights(w_ref, cells_ref, lo):
    at = slice(lo, lo + TILE)
    lx = cells_ref[0:1, at] & (BX - 1)
    ly = cells_ref[1:2, at] & (BY - 1)
    lx = jnp.broadcast_to(lx, (8, TILE))
    dy = lax.broadcasted_iota(jnp.int32, (8, TILE), 0) - ly
    on_y = [dy == j for j in range(4)]
    on_x = [lx == x for x in range(BX)]
    zero = jnp.zeros((8, TILE), F32)
    rows = [[None] * 4 for _ in range(4)]
    for i in range(4):
        for k in range(4):
            value = zero
            for j in range(4):
                row = jnp.broadcast_to(w_ref[16 * i + 4 * j + k : 16 * i + 4 * j + k + 1, at], (8, TILE))
                value = jnp.where(on_y[j], row, value)
            rows[i][k] = value
    spread = [[None] * 4 for _ in range(EX)]
    for x in range(EX):
        for k in range(4):
            value = zero
            for i in range(4):
                if 0 <= x - i < BX:
                    value = jnp.where(on_x[x - i], rows[i][k], value)
            spread[x][k] = value
    return spread


def z_hits(cells_ref, lo, k):
    bz = cells_ref[2:3, lo : lo + TILE]
    z = lax.broadcasted_iota(jnp.int32, (MESH, TILE), 0)
    return jnp.where(z == ((bz + k) & (MESH - 1)), 1.0, 0.0).astype(BF16)


def scatter_kernel(cot_ref, w_ref, cells_ref, mh_ref, ml_ref, out_ref, gh_ref, gl_ref, hit_ref, den_ref):
    atoms = cot_ref.shape[1]
    for t in range(atoms // TILE):
        lo = t * TILE
        slot = t % 2
        spread = atom_weights(w_ref, cells_ref, lo)
        for k in range(4):
            hit_ref[slot, :, k * TILE : (k + 1) * TILE] = z_hits(cells_ref, lo, k)
        for c in range(0, CH, 2):
            cots = [jnp.broadcast_to(cot_ref[c + h : c + h + 1, lo : lo + TILE], (8, TILE)) for h in range(2)]
            for k in range(4):
                g = jnp.concatenate([spread[x][k] * cots[h] for h in range(2) for x in range(EX)], axis=0)
                high, low = split(g)
                gh_ref[slot, c * ROWS : (c + 2) * ROWS, k * TILE : (k + 1) * TILE] = high
                gl_ref[slot, c * ROWS : (c + 2) * ROWS, k * TILE : (k + 1) * TILE] = low
        hit = hit_ref[slot]
        part = mm(gh_ref[slot], hit, ((1,), (1,))) + mm(gl_ref[slot], hit, ((1,), (1,)))
        if t == 0:
            den_ref[...] = part
        else:
            den_ref[...] += part
    for c in range(CH):
        rows = jnp.concatenate([den_ref[c * ROWS : (c + 1) * ROWS, :], jnp.zeros((LANES - ROWS, MESH), F32)], axis=0)
        high, low = split(rows)
        nt = ((1,), (1,))
        out_ref[c * 128 : (c + 1) * 128, :] = (
            mm(mh_ref[...], high, nt) + mm(ml_ref[...], high, nt) + mm(mh_ref[...], low, nt)
        )


def plane_kernel(in_ref, filt_ref, fh_ref, fl_ref, tw_ref, sh_ref, sl_ref, th_ref, tl_ref, lh_ref, ll_ref, out_ref):
    rows = []
    for p4 in range(PY // 4):
        high, low = split(in_ref[256 * p4 : 256 * (p4 + 1), :])
        part = mm(fh_ref[...], high) + mm(fl_ref[...], high) + mm(fh_ref[...], low)
        for p in range(4):
            rows.append((part[64 * p : 64 * p + 32], part[64 * p + 32 : 64 * p + 64]))
    rows = fft16(rows, -1)
    turned = []
    for k in range(PY):
        at = slice(PZ * k, PZ * (k + 1))
        tr, ti = tw_ref[0, at, :], tw_ref[1, at, :]
        re, im = rows[k]
        turned.append(jnp.concatenate([re * tr - im * ti, im * tr + re * ti], axis=1))
    high, low = split(jnp.concatenate(turned, axis=0))
    spec = mm(high, sh_ref[...]) + mm(high, sl_ref[...]) + mm(low, sh_ref[...])
    high, low = split(spec * filt_ref[...])
    both = mm(high, th_ref[...]) + mm(high, tl_ref[...]) + mm(low, th_ref[...])
    back = []
    for k in range(PY):
        at = slice(PZ * k, PZ * (k + 1))
        tr, ti = tw_ref[0, at, :], tw_ref[1, at, :]
        cols = []
        for ab in range(2):
            re, im = both[at, 256 * ab : 256 * ab + 128], both[at, 256 * ab + 128 : 256 * ab + 256]
            cols.append((re * tr + im * ti, im * tr - re * ti))
        back.append(cols)
    a = fft16([cols[0] for cols in back], 1)
    b = fft16([cols[1] for cols in back], 1)
    for p in range(0, PY, 2):
        stack = jnp.concatenate([a[p][0], a[p][1], b[p][0], b[p][1], a[p + 1][0], a[p + 1][1], b[p + 1][0], b[p + 1][1]], axis=0)
        high, low = split(stack)
        out_ref[64 * p : 64 * (p + 2), :] = mm(lh_ref[...], high) + mm(ll_ref[...], high) + mm(lh_ref[...], low)


def gather_kernel(in_ref, w_ref, cells_ref, bh_ref, bl_ref, out_ref, pot_ref, hit_ref, near_ref):
    atoms = out_ref.shape[1]
    for c in range(0, CH, 2):
        pots = []
        for h in range(2):
            high, low = split(in_ref[(c + h) * 128 : (c + h + 1) * 128, :].T)
            pot = mm(high, bh_ref[...]) + mm(high, bl_ref[...]) + mm(low, bh_ref[...])
            pots.append(pot[:ROWS])
        high, low = split(jnp.concatenate(pots, axis=0))
        pot_ref[c * ROWS : (c + 2) * ROWS, 0:MESH] = high
        pot_ref[c * ROWS : (c + 2) * ROWS, MESH : 2 * MESH] = low
    for t in range(atoms // TILE):
        lo = t * TILE
        slot = t % 2
        spread = atom_weights(w_ref, cells_ref, lo)
        for k in range(4):
            hit = z_hits(cells_ref, lo, k)
            hit_ref[slot, 0:MESH, k * TILE : (k + 1) * TILE] = hit
            hit_ref[slot, MESH : 2 * MESH, k * TILE : (k + 1) * TILE] = hit
        near_ref[slot] = mm(pot_ref[...], hit_ref[slot])
        for c in range(CH):
            total = jnp.zeros((8, TILE), F32)
            for x in range(EX):
                for k in range(4):
                    r = c * ROWS + 8 * x
                    total = total + spread[x][k] * near_ref[slot, r : r + 8, k * TILE : (k + 1) * TILE]
            out_ref[c : c + 1, lo : lo + TILE] = jnp.sum(total, axis=0, keepdims=True)


VMEM = pl.BlockSpec(memory_space=pltpu.VMEM)


def call(kernel, out_shape, scratch, flops, moved, *args):
    return pl.pallas_call(
        kernel,
        out_shape=jax.ShapeDtypeStruct(out_shape, F32),
        in_specs=[VMEM] * len(args),
        out_specs=VMEM,
        scratch_shapes=scratch,
        compiler_params=pltpu.CompilerParams(vmem_limit_bytes=40 * 1024 * 1024),
        cost_estimate=pl.CostEstimate(flops=flops, bytes_accessed=moved, transcendentals=0),
    )(*args)


def scatter(cotangent, spline_weights, base_cells):
    forth, _ = z_tables()
    scratch = [
        pltpu.VMEM((2, CH * ROWS, 4 * TILE), BF16),
        pltpu.VMEM((2, CH * ROWS, 4 * TILE), BF16),
        pltpu.VMEM((2, MESH, 4 * TILE), BF16),
        pltpu.VMEM((CH * ROWS, MESH), F32),
    ]
    return call(scatter_kernel, (CH * 128, LANES), scratch, 3 * 10**9, 10**6, cotangent, spline_weights, base_cells, *halves(forth))


def plane(blocks, filt):
    first, twist, second, third, last = plane_tables()
    return call(
        plane_kernel, (PY * PZ * 2, LANES), [], 10**9, 2 * 10**6,
        blocks, filt, *halves(first), twist, *halves(second), *halves(third), *halves(last),
    )


def gather(blocks, spline_weights, base_cells):
    _, back = z_tables()
    atoms = spline_weights.shape[1]
    scratch = [
        pltpu.VMEM((CH * ROWS, 2 * MESH), BF16),
        pltpu.VMEM((2, 2 * MESH, 4 * TILE), BF16),
        pltpu.VMEM((2, CH * ROWS, 4 * TILE), F32),
    ]
    return call(gather_kernel, (CH, atoms), scratch, 3 * 10**9, 10**6, blocks, spline_weights, base_cells, *halves(back))


def plane_filter(spectral_filter):
    q = lax.axis_index("pz")
    half = PZ // 2
    mine = jnp.where(q >= half, spectral_filter[:, 1:3], spectral_filter[:, 0:2])
    top = lax.ppermute(spectral_filter[:, 0], "pz", [(half, 0)])
    other = jnp.where(q == 0, top, mine[:, 0])
    other = jnp.stack([other, mine[:, 1]], axis=1)
    both = jnp.stack([mine, other], axis=2).reshape(PY, 2, BX, MESH)
    both = lax.all_to_all(both, "py", 0, 0)
    both = both.reshape(4, 4, 2, 8, 8, 16).transpose(5, 1, 3, 2, 4, 0).reshape(PY * PZ, 2, 1, 32)
    return jnp.broadcast_to(both, (PY * PZ, 2, 2, 32)).reshape(PY * PZ, 128)


def exchange(blocks):
    return lax.all_to_all(blocks.reshape(PY * PZ, 2, LANES), ("py", "pz"), 0, 0).reshape(PY * PZ * 2, LANES)


def on_device(cotangent, spline_weights, base_cells, spectral_filter):
    filt = plane_filter(spectral_filter)
    blocks = scatter(cotangent, spline_weights, base_cells)
    blocks = exchange(blocks)
    blocks = plane(blocks, filt)
    blocks = exchange(blocks)
    return gather(blocks, spline_weights, base_cells)


def solution(mesh):
    return jax.shard_map(
        on_device,
        mesh=mesh,
        in_specs=(
            P(None, ("py", "pz")),
            P(None, ("py", "pz")),
            P(None, ("py", "pz")),
            P(None, "pz", "py", None),
        ),
        out_specs=P(None, ("py", "pz")),
        check_vma=False,
    )
```

time: 872 us -> 102 us (0.12); the launches traced: 862 us -> 101 us
  other arithmetic: 399 us -> 1.61 us
  local copies, waits for them, and re-layouts: 324 us -> 11.2 us
  starting transfers between devices: 66.1 us -> 21.9 us
  waiting for transfers between devices: 54.6 us -> 22.4 us
  blocking collectives: 0 us -> 30.7 us
  matrix products: 17.3 us -> 0 us
  Pallas kernels: 0 us -> 13.3 us
    scatter-add x4 -> x0, other arithmetic: 361 us -> none  [on_device(): extended.at[:, cells.reshape(-1)].add(values.reshape(channels, -1))]
    gather x4 -> x0, local copies, waits for them, and re-layouts: 227 us -> none  [on_device(): picked = widened[:, cells]]
    unnamed x40 -> x36, local copies, waits for them, and re-layouts: 48.8 us -> 4.01 us
    all_to_all x8 -> x2, starting transfers between devices: 51.4 us -> 20.6 us  [the longest x1 10.9 us: plane_filter(): both = lax.all_to_all(both, 'py', 0, 0)]
    all_to_all x0 -> x1, blocking collectives: none -> 30.7 us  [exchange(): lax.all_to_all(blocks.reshape(PY * PZ, 2, LANES), ('py', 'pz'), 0, 0)]
    all_to_all x19 -> x0, local copies, waits for them, and re-layouts: 26.9 us -> none  [the longest x2 5.22 us: on_device(): lax.all_to_all(back_imag, 'py', split_axis=3, concat_axis=2, tiled=True)]
    ppermute x4 -> x1, waiting for transfers between devices: 28.9 us -> 6.69 us  [plane_filter(): top = lax.ppermute(spectral_filter[:, 0], 'pz', [(half, 0)])]
    dot_general x20 -> x0, matrix products: 17.3 us -> none  [the longest x1 4.07 us: on_device(): jnp.einsum('czxy,zn->cxyn', first, cos_back, precision=exact_mode)]
  transfers between devices with their start and end apart: 12 -> 3, of which waited for: 10 -> 2; matrix products, arithmetic and copies ran while one was open for 5% -> 7% of each run, Pallas kernels for 0% -> 8%
where the time goes in v1:
time: 102 us; the launch traced here: 101 us
  blocking collectives  30.7 us (30%)
  waiting for transfers between devices  22.4 us (22%)
  starting transfers between devices  21.9 us (21%)
  Pallas kernels  13.3 us (13%)
  local copies, waits for them, and re-layouts  11.2 us (11%)
  other arithmetic  1.61 us (2%)
    all_to_all x1, blocking collectives, exchange(): lax.all_to_all(blocks.reshape(PY * PZ, 2, LANES), ('py', 'pz'), 0, 0)  30.7 us
    all_to_all x1, waiting for transfers between devices, exchange(): lax.all_to_all(blocks.reshape(PY * PZ, 2, LANES), ('py', 'pz'), 0, 0)  15.7 us
    pallas_call x3, Pallas kernels, call(): pl.pallas_call(kernel, out_shape=jax.ShapeDtypeStruct(out_shape, F32), in...  13.3 us
    all_to_all x1, starting transfers between devices, plane_filter(): both = lax.all_to_all(both, 'py', 0, 0)  10.9 us
    all_to_all x1, starting transfers between devices, exchange(): lax.all_to_all(blocks.reshape(PY * PZ, 2, LANES), ('py', 'pz'), 0, 0)  9.66 us
    ppermute x1, waiting for transfers between devices, plane_filter(): top = lax.ppermute(spectral_filter[:, 0], 'pz', [(half, 0)])  6.69 us
    broadcast_in_dim x2, local copies, waits for them, and re-layouts, plane_filter(): return jnp.broadcast_to(both, (PY * PZ, 2, 2, 32)).reshape(PY * PZ, 128)  4.15 us
    unnamed x36, local copies, waits for them, and re-layouts  4.01 us
  transfers between devices with their start and end apart: 3, of which 2 were waited for; matrix products, arithmetic and copies ran while one was open for 7% of the time, Pallas kernels for 8%

profile of v1, /device:TPU:1, one launch (start us, length us, event | category | flops | bytes accessed | tf_op | source)
XLA Modules:
  0.0 101.2 jit_solution(11968692124255135583)
XLA Ops:
  0.0 0.8 slice_bitcast_fusion.1
  0.8 1.3 %collective-permute-start = (f32[8,8,128]{2,1,0:T(8,128)S(1)}, f32[8,8,128]{2,1,0:T(8,128)S(1)}, u32[]{:S(2)}, u32[]{:S(2)}) collective-permute-start(f32[8,8,128]{2,1,0:T(8,128)S(1)} %slice_bitcast_fusion.1), channel_id=1, source_target_pairs={{16,0},{48,32},{80,64},{112,96},{144,128},{176,160},{208,192},{240... | collective-permute-start | bytes 98312 | tf_op jit(solution)/shard_map/ppermute | solution.py:325
  2.1 0.9 slice_select_fusion
  3.0 6.7 %collective-permute-done = f32[8,8,128]{2,1,0:T(8,128)S(1)} collective-permute-done((f32[8,8,128]{2,1,0:T(8,128)S(1)}, f32[8,8,128]{2,1,0:T(8,128)S(1)}, u32[]{:S(2)}, u32[]{:S(2)}) %collective-permute-start) | collective-permute-done | bytes 32800 | tf_op jit(solution)/shard_map/ppermute | solution.py:325
  9.7 0.7 pad_maximum_fusion
  10.4 10.9 %all-to-all-start.1 = ((f32[16,2,8,128]{3,2,1,0:T(8,128)}), f32[16,2,8,128]{3,2,1,0:T(8,128)S(1)}, u32[]{:S(2)}, u32[]{:S(2)}) async-start(f32[16,2,8,128]{3,2,1,0:T(8,128)} %pad_maximum_fusion), calls=%async_computation.1 | async-start | bytes 262144 | tf_op jit(solution)/shard_map/all_to_all | solution.py:329
  21.3 0.0 copy-start
  21.3 0.9 copy-done
  22.3 0.0 copy-start.2
  22.3 0.8 copy-done.2
  23.0 0.0 copy-start.3
  23.0 0.7 copy-done.3
  23.8 0.0 copy-start.16
  23.8 0.8 copy-done.16
  24.5 0.0 copy-start.17
  24.5 0.8 copy-done.17
  25.3 7.6 %shard_map.163 = f32[1024,128]{1,0:T(8,128)} custom-call(f32[8,1024]{1,0:T(8,128)S(1)} %copy-done.2, f32[64,1024]{1,0:T(8,128)S(1)} %copy-done, s32[3,1024]{1,0:T(4,128)S(1)} %copy-done.3, bf16[128,128]{1,0:T(8,128)(2,1)S(1)} %copy-done.16, bf16[128,128]{1,0:T(8,128)(2,1)S(1)} %copy-done.17), custom_call_target="tpu_custom_call" | custom-call | flops 3000000000 | bytes 1000000 | tf_op jit(solution)/shard_map/pallas_call | solution.py:280
  32.9 0.0 all-to-all-done.1
  32.9 9.7 %all-to-all-start = ((f32[512,2,128]{2,1,0:T(2,128)}), f32[512,2,128]{2,1,0:T(2,128)S(1)}, u32[]{:S(2)}, u32[]{:S(2)}) async-start(f32[512,2,128]{2,1,0:T(2,128)} %bitcast), calls=%async_computation | async-start | bytes 1048576 | tf_op jit(solution)/shard_map/all_to_all | solution.py:335
  42.6 0.3 reshape.27
  42.9 1.8 %copy.28 = f32[16,4,8,2,8,4]{2,1,0,5,4,3:T(4,128)} copy(f32[16,4,8,2,8,4]{0,4,2,3,1,5:T(8,128)S(1)} %bitcast.33) | data formatting | bytes 262144 | tf_op jit(solution)/shard_map/transpose | solution.py:330
  44.7 0.0 copy-start.5
  44.7 0.0 copy-start.6
  44.7 0.0 copy-start.7
  44.7 0.0 copy-start.8
  44.7 0.0 copy-start.9
  44.7 0.0 copy-start.10
  44.7 0.0 copy-start.11
  44.7 0.0 copy-start.12
  44.8 0.0 copy-start.13
  44.8 4.1 %broadcast_in_dim.7 = f32[512,2,32]{0,2,1:T(8,128)S(1)} reshape(f32[16,4,8,2,8,4]{2,1,0,5,4,3:T(4,128)} %copy.28) | data formatting | bytes 262144 | tf_op jit(solution)/shard_map/broadcast_in_dim | solution.py:331
  48.9 0.1 copy.29.filt_ref
  49.1 15.7 %all-to-all-done = f32[512,2,128]{2,1,0:T(2,128)S(1)} async-done(((f32[512,2,128]{2,1,0:T(2,128)}), f32[512,2,128]{2,1,0:T(2,128)S(1)}, u32[]{:S(2)}, u32[]{:S(2)}) %all-to-all-start) | async-done | bytes 524320 | tf_op jit(solution)/shard_map/all_to_all | solution.py:335
  64.8 0.0 copy-done.5
  64.8 0.0 copy-done.6
  64.8 0.0 copy-done.7
  64.8 0.0 copy-done.8
  64.8 0.0 copy-done.9
  64.8 0.0 copy-done.10
  64.8 0.0 copy-done.11
  64.8 0.0 copy-done.12
  64.8 0.0 copy-done.13
  64.8 0.0 copy-start.1
  64.8 0.0 copy-start.4
  64.9 0.0 copy-start.14
  64.9 0.0 copy-start.15
  64.9 2.8 %shard_map.164 = f32[1024,128]{1,0:T(8,128)S(1)} custom-call(f32[1024,128]{1,0:T(8,128)S(1)} %bitcast.30, f32[512,128]{1,0:T(8,128)S(1)} %copy.29.filt_ref, bf16[256,256]{1,0:T(8,128)(2,1)S(1)} %copy-done.6, bf16[256,256]{1,0:T(8,128)(2,1)S(1)} %copy-done.7, f32[2,512,128]{2,1,0:T(8,128)S(1)} %copy-done.5, bf16[256,128]{1,0:T(8,128)(2,1)S(1)} %copy-done.10, ...), custom_call_target="tpu_custom_call" | custom-call | flops 1000000000 | bytes 2000000 | tf_op jit(solution)/shard_map/pallas_call | solution.py:280
  67.7 30.7 %all_to_all.15 = f32[512,2,128]{2,1,0:T(2,128)S(1)} all-to-all(f32[512,2,128]{2,1,0:T(2,128)S(1)} %bitcast.31), channel_id=1, replica_groups=mesh['py'=16,'pz'=32] {'py','pz'}, dimensions={0} | all-to-all | bytes 1048576 | tf_op jit(solution)/shard_map/all_to_all | solution.py:335
  98.3 0.0 copy-done.1
  98.4 0.0 copy-done.4
  98.4 0.0 copy-done.14
  98.4 0.0 copy-done.15
  98.4 2.9 %shard_map.165 = f32[8,1024]{1,0:T(8,128)} custom-call(f32[1024,128]{1,0:T(8,128)S(1)} %bitcast.32, f32[64,1024]{1,0:T(8,128)S(1)} %copy-done.1, s32[3,1024]{1,0:T(4,128)S(1)} %copy-done.4, bf16[128,128]{1,0:T(8,128)(2,1)S(1)} %copy-done.14, bf16[128,128]{1,0:T(8,128)(2,1)S(1)} %copy-done.15), custom_call_target="tpu_custom_call" | custom-call | flops 3000000000 | bytes 1000000 | tf_op jit(solution)/shard_map/pallas_call | solution.py:280
  (4 shorter events, 0.0 us)
Async XLA Ops:
  0.8 8.9 %collective-permute-start = (f32[8,8,128]{2,1,0:T(8,128)S(1)}, f32[8,8,128]{2,1,0:T(8,128)S(1)}, u32[]{:S(2)}, u32[]{:S(2)}) collective-permute-start(f32[8,8,128]{2,1,0:T(8,128)S(1)} %slice_bitcast_fusion.1), channel_id=1, source_target_pairs={{16,0},{48,32},{80,64},{112,96},{144,128},{176,160},{208,192},{240... | collective-permute-start | bytes 98312 | tf_op jit(solution)/shard_map/ppermute | solution.py:325
  10.4 22.5 %all-to-all-start.1 = ((f32[16,2,8,128]{3,2,1,0:T(8,128)}), f32[16,2,8,128]{3,2,1,0:T(8,128)S(1)}, u32[]{:S(2)}, u32[]{:S(2)}) async-start(f32[16,2,8,128]{3,2,1,0:T(8,128)} %pad_maximum_fusion), calls=%async_computation.1 | async-start | bytes 262144 | tf_op jit(solution)/shard_map/all_to_all | solution.py:329
  21.3 0.9 copy-start
  22.3 0.8 copy-start.2
  23.0 0.7 copy-start.3
  23.8 0.8 copy-start.16
  24.5 0.8 copy-start.17
  32.9 31.9 %all-to-all-start = ((f32[512,2,128]{2,1,0:T(2,128)}), f32[512,2,128]{2,1,0:T(2,128)S(1)}, u32[]{:S(2)}, u32[]{:S(2)}) async-start(f32[512,2,128]{2,1,0:T(2,128)} %bitcast), calls=%async_computation | async-start | bytes 1048576 | tf_op jit(solution)/shard_map/all_to_all | solution.py:335
  44.7 20.1 %copy-start.5 = (f32[2,512,128]{2,1,0:T(8,128)S(1)}, f32[2,512,128]{2,1,0:T(8,128)}, u32[]{:S(2)}) copy-start(f32[2,512,128]{2,1,0:T(8,128)} %constant.38.clone.tw_ref) | copy-start | bytes 1572868
  44.7 20.1 %copy-start.6 = (bf16[256,256]{1,0:T(8,128)(2,1)S(1)}, bf16[256,256]{1,0:T(8,128)(2,1)}, u32[]{:S(2)}) copy-start(bf16[256,256]{1,0:T(8,128)(2,1)} %constant.36.clone.fh_ref) | copy-start | bytes 393220
  44.7 20.1 %copy-start.7 = (bf16[256,256]{1,0:T(8,128)(2,1)S(1)}, bf16[256,256]{1,0:T(8,128)(2,1)}, u32[]{:S(2)}) copy-start(bf16[256,256]{1,0:T(8,128)(2,1)} %constant.37.clone.fl_ref) | copy-start | bytes 393220
  44.7 20.1 %copy-start.8 = (bf16[128,512]{1,0:T(8,128)(2,1)S(1)}, bf16[128,512]{1,0:T(8,128)(2,1)}, u32[]{:S(2)}) copy-start(bf16[128,512]{1,0:T(8,128)(2,1)} %constant.41.clone.th_ref) | copy-start | bytes 393220
  44.7 20.1 %copy-start.9 = (bf16[128,512]{1,0:T(8,128)(2,1)S(1)}, bf16[128,512]{1,0:T(8,128)(2,1)}, u32[]{:S(2)}) copy-start(bf16[128,512]{1,0:T(8,128)(2,1)} %constant.42.clone.tl_ref) | copy-start | bytes 393220
  44.7 20.1 %copy-start.10 = (bf16[256,128]{1,0:T(8,128)(2,1)S(1)}, bf16[256,128]{1,0:T(8,128)(2,1)}, u32[]{:S(2)}) copy-start(bf16[256,128]{1,0:T(8,128)(2,1)} %constant.39.clone.sh_ref) | copy-start | bytes 196612
  44.7 20.1 %copy-start.11 = (bf16[256,128]{1,0:T(8,128)(2,1)S(1)}, bf16[256,128]{1,0:T(8,128)(2,1)}, u32[]{:S(2)}) copy-start(bf16[256,128]{1,0:T(8,128)(2,1)} %constant.40.clone.sl_ref) | copy-start | bytes 196612
  44.7 20.1 %copy-start.12 = (bf16[128,256]{1,0:T(8,128)(2,1)S(1)}, bf16[128,256]{1,0:T(8,128)(2,1)}, u32[]{:S(2)}) copy-start(bf16[128,256]{1,0:T(8,128)(2,1)} %constant.43.clone.lh_ref) | copy-start | bytes 196612
  44.8 20.1 %copy-start.13 = (bf16[128,256]{1,0:T(8,128)(2,1)S(1)}, bf16[128,256]{1,0:T(8,128)(2,1)}, u32[]{:S(2)}) copy-start(bf16[128,256]{1,0:T(8,128)(2,1)} %constant.44.clone.ll_ref) | copy-start | bytes 196612
  64.8 33.5 %copy-start.1 = (f32[64,1024]{1,0:T(8,128)S(1)}, f32[64,1024]{1,0:T(8,128)}, u32[]{:S(2)}) copy-start(f32[64,1024]{1,0:T(8,128)} %w_ref.3) | copy-start | bytes 786436
  64.8 33.5 %copy-start.4 = (s32[3,1024]{1,0:T(4,128)S(1)}, s32[3,1024]{1,0:T(4,128)}, u32[]{:S(2)}) copy-start(s32[3,1024]{1,0:T(4,128)} %cells_ref.3) | copy-start | bytes 36868
  64.9 33.5 %copy-start.14 = (bf16[128,128]{1,0:T(8,128)(2,1)S(1)}, bf16[128,128]{1,0:T(8,128)(2,1)}, u32[]{:S(2)}) copy-start(bf16[128,128]{1,0:T(8,128)(2,1)} %constant.45.clone.bh_ref) | copy-start | bytes 98308
  64.9 33.5 %copy-start.15 = (bf16[128,128]{1,0:T(8,128)(2,1)S(1)}, bf16[128,128]{1,0:T(8,128)(2,1)}, u32[]{:S(2)}) copy-start(bf16[128,128]{1,0:T(8,128)(2,1)} %constant.46.clone.bl_ref) | copy-start | bytes 98308

commit v2 on v1

--- a/solution.py
+++ b/solution.py
@@ -42,17 +42,17 @@
     scale = 1.0 / float(MESH) ** 3
     for s in range(2):
         for q in range(PZ):
-            kz = 4 * q + s + (1 if q >= PZ // 2 else 0)
+            kz = 4 * q + 2 * s + (1 if q < PZ // 2 else 0)
             wave = turn(kz * z, MESH)
             forth[s, q, 0] = wave.real
             forth[s, q, 1] = -wave.imag
             back[s, q, 0] = 2.0 * scale * wave.real
             back[s, q, 1] = -2.0 * scale * wave.imag
     sign = 1.0 - 2.0 * (z % 2)
-    forth[0, 0, 0] = 1.0
-    forth[0, 0, 1] = sign
-    back[0, 0, 0] = scale
-    back[0, 0, 1] = scale * sign
+    forth[0, PZ // 2, 0] = 1.0
+    forth[0, PZ // 2, 1] = sign
+    back[0, PZ // 2, 0] = scale
+    back[0, PZ // 2, 1] = scale * sign
     return forth.reshape(128, MESH), back.reshape(128, MESH)
 
 
@@ -179,33 +179,45 @@
     return jnp.where(z == ((bz + k) & (MESH - 1)), 1.0, 0.0).astype(BF16)
 
 
-def scatter_kernel(cot_ref, w_ref, cells_ref, mh_ref, ml_ref, out_ref, gh_ref, gl_ref, hit_ref, den_ref):
+def scatter_kernel(cot_in, w_in, cells_in, m_in, out_ref, cot_ref, w_ref, cells_ref, m_ref, hit_ref, den_ref, sems):
+    pairs = ((cells_in, cells_ref), (cot_in, cot_ref), (w_in, w_ref), (m_in, m_ref))
+    copies = [pltpu.make_async_copy(a, b, sems.at[i]) for i, (a, b) in enumerate(pairs)]
+    for copy in copies:
+        copy.start()
+    for copy in copies[:3]:
+        copy.wait()
     atoms = cot_ref.shape[1]
     for t in range(atoms // TILE):
         lo = t * TILE
         slot = t % 2
         spread = atom_weights(w_ref, cells_ref, lo)
+        bz = jnp.broadcast_to(cells_ref[2:3, lo : lo + TILE], (TILE, TILE)).T
+        zz = lax.broadcasted_iota(jnp.int32, (TILE, MESH), 1)
         for k in range(4):
-            hit_ref[slot, :, k * TILE : (k + 1) * TILE] = z_hits(cells_ref, lo, k)
+            hit_ref[slot, k * TILE : (k + 1) * TILE, :] = jnp.where(zz == ((bz + k) & (MESH - 1)), 1.0, 0.0).astype(BF16)
+        hit = hit_ref[slot]
         for c in range(0, CH, 2):
             cots = [jnp.broadcast_to(cot_ref[c + h : c + h + 1, lo : lo + TILE], (8, TILE)) for h in range(2)]
+            hs, ls = [], []
             for k in range(4):
                 g = jnp.concatenate([spread[x][k] * cots[h] for h in range(2) for x in range(EX)], axis=0)
                 high, low = split(g)
-                gh_ref[slot, c * ROWS : (c + 2) * ROWS, k * TILE : (k + 1) * TILE] = high
-                gl_ref[slot, c * ROWS : (c + 2) * ROWS, k * TILE : (k + 1) * TILE] = low
-        hit = hit_ref[slot]
-        part = mm(gh_ref[slot], hit, ((1,), (1,))) + mm(gl_ref[slot], hit, ((1,), (1,)))
-        if t == 0:
-            den_ref[...] = part
-        else:
-            den_ref[...] += part
+                hs.append(high)
+                ls.append(low)
+            part = mm(jnp.concatenate(hs, axis=1), hit) + mm(jnp.concatenate(ls, axis=1), hit)
+            at = slice(c * ROWS, (c + 2) * ROWS)
+            if t == 0:
+                den_ref[at, :] = part
+            else:
+                den_ref[at, :] += part
+    copies[3].wait()
+    mh, ml = m_ref[0], m_ref[1]
     for c in range(CH):
         rows = jnp.concatenate([den_ref[c * ROWS : (c + 1) * ROWS, :], jnp.zeros((LANES - ROWS, MESH), F32)], axis=0)
         high, low = split(rows)
         nt = ((1,), (1,))
         out_ref[c * 128 : (c + 1) * 128, :] = (
-            mm(mh_ref[...], high, nt) + mm(ml_ref[...], high, nt) + mm(mh_ref[...], low, nt)
+            mm(mh, high, nt) + mm(ml, high, nt) + mm(mh, low, nt)
         )
 
 
@@ -273,30 +285,28 @@
             out_ref[c : c + 1, lo : lo + TILE] = jnp.sum(total, axis=0, keepdims=True)
 
 
-VMEM = pl.BlockSpec(memory_space=pltpu.VMEM)
-
-
-def call(kernel, out_shape, scratch, flops, moved, *args):
+def call(kernel, out_shape, scratch, flops, moved, *args, space=pltpu.VMEM, limit=40):
     return pl.pallas_call(
         kernel,
         out_shape=jax.ShapeDtypeStruct(out_shape, F32),
-        in_specs=[VMEM] * len(args),
-        out_specs=VMEM,
+        in_specs=[pl.BlockSpec(memory_space=space)] * len(args),
+        out_specs=pl.BlockSpec(memory_space=pltpu.VMEM),
         scratch_shapes=scratch,
-        compiler_params=pltpu.CompilerParams(vmem_limit_bytes=40 * 1024 * 1024),
+        compiler_params=pltpu.CompilerParams(vmem_limit_bytes=limit * 1024 * 1024),
         cost_estimate=pl.CostEstimate(flops=flops, bytes_accessed=moved, transcendentals=0),
     )(*args)
 
 
 def scatter(cotangent, spline_weights, base_cells):
     forth, _ = z_tables()
-    scratch = [
-        pltpu.VMEM((2, CH * ROWS, 4 * TILE), BF16),
-        pltpu.VMEM((2, CH * ROWS, 4 * TILE), BF16),
-        pltpu.VMEM((2, MESH, 4 * TILE), BF16),
+    table = np.stack(halves(forth))
+    args = (cotangent, spline_weights, base_cells, table)
+    scratch = [pltpu.VMEM(a.shape, a.dtype) for a in args] + [
+        pltpu.VMEM((2, 4 * TILE, MESH), BF16),
         pltpu.VMEM((CH * ROWS, MESH), F32),
+        pltpu.SemaphoreType.DMA((4,)),
     ]
-    return call(scatter_kernel, (CH * 128, LANES), scratch, 3 * 10**9, 10**6, cotangent, spline_weights, base_cells, *halves(forth))
+    return call(scatter_kernel, (CH * 128, LANES), scratch, 3 * 10**9, 10**6, *args, space=pltpu.HBM, limit=60)
 
 
 def plane(blocks, filt):
@@ -319,14 +329,13 @@
 
 
 def plane_filter(spectral_filter):
-    q = lax.axis_index("pz")
+    p, q = lax.axis_index("py"), lax.axis_index("pz")
     half = PZ // 2
-    mine = jnp.where(q >= half, spectral_filter[:, 1:3], spectral_filter[:, 0:2])
-    top = lax.ppermute(spectral_filter[:, 0], "pz", [(half, 0)])
-    other = jnp.where(q == 0, top, mine[:, 0])
-    other = jnp.stack([other, mine[:, 1]], axis=1)
-    both = jnp.stack([mine, other], axis=2).reshape(PY, 2, BX, MESH)
-    both = lax.all_to_all(both, "py", 0, 0)
+    pair = lax.all_to_all(spectral_filter.reshape(PY, 2, BX, MESH), "py", 0, 0)
+    even = lax.ppermute(pair[:, 0], "pz", [(0, half)])
+    mine = jnp.where(q < half, pair[:, 1], pair[:, 0])
+    shared = (q == half) & (p % 2 == 0)
+    both = jnp.stack([jnp.where(shared, even, mine), mine], axis=1)
     both = both.reshape(4, 4, 2, 8, 8, 16).transpose(5, 1, 3, 2, 4, 0).reshape(PY * PZ, 2, 1, 32)
     return jnp.broadcast_to(both, (PY * PZ, 2, 2, 32)).reshape(PY * PZ, 128)
 

time: 102 us -> 93.5 us (0.917)
  waiting for transfers between devices: 22.4 us -> 8.2 us
  starting transfers between devices: 21.9 us -> 35.1 us
  local copies, waits for them, and re-layouts: 11.2 us -> 6.56 us
  Pallas kernels: 13.3 us -> 11.6 us
  other arithmetic: 1.61 us -> 0.13 us
    all_to_all x1, waiting for transfers between devices: 15.7 us -> 6.28 us  [exchange(): lax.all_to_all(blocks.reshape(PY * PZ, 2, LANES), ('py', 'pz'), 0, 0)]
    all_to_all x1, starting transfers between devices: 9.66 us -> 17.4 us  [exchange(): lax.all_to_all(blocks.reshape(PY * PZ, 2, LANES), ('py', 'pz'), 0, 0)]
    ppermute x1, starting transfers between devices: 1.28 us -> 7.5 us  [plane_filter(): even = lax.ppermute(pair[:, 0], 'pz', [(0, half)])]
    ppermute x1, waiting for transfers between devices: 6.69 us -> 1.63 us  [plane_filter(): even = lax.ppermute(pair[:, 0], 'pz', [(0, half)])]
    unnamed x36 -> x26, local copies, waits for them, and re-layouts: 4.01 us -> 0.08 us
    pallas_call x3, Pallas kernels: 13.3 us -> 11.6 us  [call(): pl.pallas_call(kernel, out_shape=jax.ShapeDtypeStruct(out_shape, F32), in...]
  transfers between devices with their start and end apart: 3 -> 3, of which waited for: 2 -> 3; matrix products, arithmetic and copies ran while one was open for 7% -> 7% of each run, Pallas kernels for 8% -> 6%
where the time goes in v2:
time: 93.5 us; the launch traced here: 93.1 us
  starting transfers between devices  35.1 us (38%)
  blocking collectives  31.3 us (33%)
  Pallas kernels  11.6 us (12%)
  waiting for transfers between devices  8.2 us (9%)
  local copies, waits for them, and re-layouts  6.56 us (7%)
    all_to_all x1, blocking collectives, exchange(): lax.all_to_all(blocks.reshape(PY * PZ, 2, LANES), ('py', 'pz'), 0, 0)  31.3 us
    all_to_all x1, starting transfers between devices, exchange(): lax.all_to_all(blocks.reshape(PY * PZ, 2, LANES), ('py', 'pz'), 0, 0)  17.4 us
    pallas_call x3, Pallas kernels, call(): pl.pallas_call(kernel, out_shape=jax.ShapeDtypeStruct(out_shape, F32), in...  11.6 us
    all_to_all x1, starting transfers between devices, plane_filter(): pair = lax.all_to_all(spectral_filter.reshape(PY, 2, BX, MESH), 'py', 0, 0)  10.2 us
    ppermute x1, starting transfers between devices, plane_filter(): even = lax.ppermute(pair[:, 0], 'pz', [(0, half)])  7.5 us
    all_to_all x1, waiting for transfers between devices, exchange(): lax.all_to_all(blocks.reshape(PY * PZ, 2, LANES), ('py', 'pz'), 0, 0)  6.28 us
    broadcast_in_dim x2, local copies, waits for them, and re-layouts, plane_filter(): return jnp.broadcast_to(both, (PY * PZ, 2, 2, 32)).reshape(PY * PZ, 128)  4.15 us
  transfers between devices with their start and end apart: 3, of which 3 were waited for; matrix products, arithmetic and copies ran while one was open for 7% of the time, Pallas kernels for 6%

profile of v2, /device:TPU:1, one launch (start us, length us, event | category | flops | bytes accessed | tf_op | source)
XLA Modules:
  0.0 93.1 jit_solution(4382083072511984743)
XLA Ops:
  0.0 10.2 %all-to-all-start.1 = ((f32[16,2,8,128]{3,2,1,0:T(8,128)}), f32[16,2,8,128]{3,2,1,0:T(8,128)S(1)}, u32[]{:S(2)}, u32[]{:S(2)}) async-start(f32[16,2,8,128]{3,2,1,0:T(8,128)} %bitcast.25), calls=%async_computation.1 | async-start | bytes 262144 | tf_op jit(solution)/shard_map/all_to_all | solution.py:334
  10.2 5.9 %shard_map.154 = f32[1024,128]{1,0:T(8,128)} custom-call(f32[8,1024]{1,0:T(8,128)} %cot_in.1, f32[64,1024]{1,0:T(8,128)} %w_ref.1, s32[3,1024]{1,0:T(4,128)} %cells_ref.1, bf16[2,128,128]{2,1,0:T(8,128)(2,1)} %constant.49.clone.m_in), custom_call_target="tpu_custom_call" | custom-call | flops 3000000000 | bytes 1000000 | tf_op jit(solution)/shard_map/pallas_call | solution.py:289
  16.1 0.3 all-to-all-done.1
  16.4 17.4 %all-to-all-start = ((f32[512,2,128]{2,1,0:T(2,128)}), f32[512,2,128]{2,1,0:T(2,128)S(1)}, u32[]{:S(2)}, u32[]{:S(2)}) async-start(f32[512,2,128]{2,1,0:T(2,128)} %bitcast.24), calls=%async_computation | async-start | bytes 1048576 | tf_op jit(solution)/shard_map/all_to_all | solution.py:344
  33.9 7.5 %collective-permute-start = (f32[16,8,128]{2,1,0:T(8,128)S(1)}, f32[16,8,128]{2,1,0:T(8,128)S(1)}, u32[]{:S(2)}, u32[]{:S(2)}) collective-permute-start(f32[16,8,128]{2,1,0:T(8,128)S(1)} %get-tuple-element.5), channel_id=1, source_target_pairs={{0,16},{32,48},{64,80},{96,112},{128,144},{160,176},{192,208},{224... | collective-permute-start | bytes 196616 | tf_op jit(solution)/shard_map/ppermute | solution.py:335
  41.4 0.2 stack.10
  41.6 1.6 %collective-permute-done = f32[16,8,128]{2,1,0:T(8,128)S(1)} collective-permute-done((f32[16,8,128]{2,1,0:T(8,128)S(1)}, f32[16,8,128]{2,1,0:T(8,128)S(1)}, u32[]{:S(2)}, u32[]{:S(2)}) %collective-permute-start) | collective-permute-done | bytes 65568 | tf_op jit(solution)/shard_map/ppermute | solution.py:335
  43.2 0.2 stack.9
  43.4 0.1 maximum_bitcast_fusion
  43.5 1.8 %copy.22 = f32[16,4,8,2,8,4]{2,1,0,5,4,3:T(4,128)} copy(f32[16,4,8,2,8,4]{0,4,2,1,5,3:T(8,128)S(1)} %maximum_bitcast_fusion) | data formatting | bytes 262144 | tf_op jit(solution)/shard_map/transpose | solution.py:339
  45.4 0.0 copy-start.2
  45.4 0.0 copy-start.3
  45.4 0.0 copy-start.4
  45.4 0.0 copy-start.5
  45.4 0.0 copy-start.6
  45.4 0.0 copy-start.7
  45.4 0.0 copy-start.8
  45.4 0.0 copy-start.9
  45.5 0.0 copy-start.10
  45.5 4.1 %broadcast_in_dim.7 = f32[512,2,32]{0,2,1:T(8,128)S(1)} reshape(f32[16,4,8,2,8,4]{2,1,0,5,4,3:T(4,128)} %copy.22) | data formatting | bytes 262144 | tf_op jit(solution)/shard_map/broadcast_in_dim | solution.py:340
  49.6 0.1 copy.23.filt_ref
  49.8 6.3 %all-to-all-done = f32[512,2,128]{2,1,0:T(2,128)S(1)} async-done(((f32[512,2,128]{2,1,0:T(2,128)}), f32[512,2,128]{2,1,0:T(2,128)S(1)}, u32[]{:S(2)}, u32[]{:S(2)}) %all-to-all-start) | async-done | bytes 524320 | tf_op jit(solution)/shard_map/all_to_all | solution.py:344
  56.0 0.0 copy-done.2
  56.0 0.0 copy-done.3
  56.0 0.0 copy-done.4
  56.1 0.0 copy-done.5
  56.1 0.0 copy-done.6
  56.1 0.0 copy-done.7
  56.1 0.0 copy-done.8
  56.1 0.0 copy-done.9
  56.1 0.0 copy-done.10
  56.1 0.0 copy-start
  56.1 0.0 copy-start.1
  56.1 0.0 copy-start.11
  56.2 0.0 copy-start.12
  56.2 2.8 %shard_map.155 = f32[1024,128]{1,0:T(8,128)S(1)} custom-call(f32[1024,128]{1,0:T(8,128)S(1)} %bitcast.20, f32[512,128]{1,0:T(8,128)S(1)} %copy.23.filt_ref, bf16[256,256]{1,0:T(8,128)(2,1)S(1)} %copy-done.3, bf16[256,256]{1,0:T(8,128)(2,1)S(1)} %copy-done.4, f32[2,512,128]{2,1,0:T(8,128)S(1)} %copy-done.2, bf16[256,128]{1,0:T(8,128)(2,1)S(1)} %copy-done.7, ...), custom_call_target="tpu_custom_call" | custom-call | flops 1000000000 | bytes 2000000 | tf_op jit(solution)/shard_map/pallas_call | solution.py:289
  58.9 31.3 %all_to_all.15 = f32[512,2,128]{2,1,0:T(2,128)S(1)} all-to-all(f32[512,2,128]{2,1,0:T(2,128)S(1)} %bitcast.21), channel_id=1, replica_groups=mesh['py'=16,'pz'=32] {'py','pz'}, dimensions={0} | all-to-all | bytes 1048576 | tf_op jit(solution)/shard_map/all_to_all | solution.py:344
  90.2 0.0 copy-done
  90.2 0.0 copy-done.1
  90.2 0.0 copy-done.11
  90.3 0.0 copy-done.12
  90.3 2.9 %shard_map.156 = f32[8,1024]{1,0:T(8,128)} custom-call(f32[1024,128]{1,0:T(8,128)S(1)} %bitcast.22, f32[64,1024]{1,0:T(8,128)S(1)} %copy-done, s32[3,1024]{1,0:T(4,128)S(1)} %copy-done.1, bf16[128,128]{1,0:T(8,128)(2,1)S(1)} %copy-done.11, bf16[128,128]{1,0:T(8,128)(2,1)S(1)} %copy-done.12), custom_call_target="tpu_custom_call" | custom-call | flops 3000000000 | bytes 1000000 | tf_op jit(solution)/shard_map/pallas_call | solution.py:289
  (3 shorter events, 0.0 us)
Async XLA Ops:
  0.0 16.4 %all-to-all-start.1 = ((f32[16,2,8,128]{3,2,1,0:T(8,128)}), f32[16,2,8,128]{3,2,1,0:T(8,128)S(1)}, u32[]{:S(2)}, u32[]{:S(2)}) async-start(f32[16,2,8,128]{3,2,1,0:T(8,128)} %bitcast.25), calls=%async_computation.1 | async-start | bytes 262144 | tf_op jit(solution)/shard_map/all_to_all | solution.py:334
  16.4 39.6 %all-to-all-start = ((f32[512,2,128]{2,1,0:T(2,128)}), f32[512,2,128]{2,1,0:T(2,128)S(1)}, u32[]{:S(2)}, u32[]{:S(2)}) async-start(f32[512,2,128]{2,1,0:T(2,128)} %bitcast.24), calls=%async_computation | async-start | bytes 1048576 | tf_op jit(solution)/shard_map/all_to_all | solution.py:344
  33.9 9.3 %collective-permute-start = (f32[16,8,128]{2,1,0:T(8,128)S(1)}, f32[16,8,128]{2,1,0:T(8,128)S(1)}, u32[]{:S(2)}, u32[]{:S(2)}) collective-permute-start(f32[16,8,128]{2,1,0:T(8,128)S(1)} %get-tuple-element.5), channel_id=1, source_target_pairs={{0,16},{32,48},{64,80},{96,112},{128,144},{160,176},{192,208},{224... | collective-permute-start | bytes 196616 | tf_op jit(solution)/shard_map/ppermute | solution.py:335
  45.4 10.6 %copy-start.2 = (f32[2,512,128]{2,1,0:T(8,128)S(1)}, f32[2,512,128]{2,1,0:T(8,128)}, u32[]{:S(2)}) copy-start(f32[2,512,128]{2,1,0:T(8,128)} %constant.52.clone.tw_ref) | copy-start | bytes 1572868
  45.4 10.6 %copy-start.3 = (bf16[256,256]{1,0:T(8,128)(2,1)S(1)}, bf16[256,256]{1,0:T(8,128)(2,1)}, u32[]{:S(2)}) copy-start(bf16[256,256]{1,0:T(8,128)(2,1)} %constant.50.clone.fh_ref) | copy-start | bytes 393220
  45.4 10.6 %copy-start.4 = (bf16[256,256]{1,0:T(8,128)(2,1)S(1)}, bf16[256,256]{1,0:T(8,128)(2,1)}, u32[]{:S(2)}) copy-start(bf16[256,256]{1,0:T(8,128)(2,1)} %constant.51.clone.fl_ref) | copy-start | bytes 393220
  45.4 10.7 %copy-start.5 = (bf16[128,512]{1,0:T(8,128)(2,1)S(1)}, bf16[128,512]{1,0:T(8,128)(2,1)}, u32[]{:S(2)}) copy-start(bf16[128,512]{1,0:T(8,128)(2,1)} %constant.55.clone.th_ref) | copy-start | bytes 393220
  45.4 10.7 %copy-start.6 = (bf16[128,512]{1,0:T(8,128)(2,1)S(1)}, bf16[128,512]{1,0:T(8,128)(2,1)}, u32[]{:S(2)}) copy-start(bf16[128,512]{1,0:T(8,128)(2,1)} %constant.56.clone.tl_ref) | copy-start | bytes 393220
  45.4 10.7 %copy-start.7 = (bf16[256,128]{1,0:T(8,128)(2,1)S(1)}, bf16[256,128]{1,0:T(8,128)(2,1)}, u32[]{:S(2)}) copy-start(bf16[256,128]{1,0:T(8,128)(2,1)} %constant.53.clone.sh_ref) | copy-start | bytes 196612
  45.4 10.7 %copy-start.8 = (bf16[256,128]{1,0:T(8,128)(2,1)S(1)}, bf16[256,128]{1,0:T(8,128)(2,1)}, u32[]{:S(2)}) copy-start(bf16[256,128]{1,0:T(8,128)(2,1)} %constant.54.clone.sl_ref) | copy-start | bytes 196612
  45.4 10.6 %copy-start.9 = (bf16[128,256]{1,0:T(8,128)(2,1)S(1)}, bf16[128,256]{1,0:T(8,128)(2,1)}, u32[]{:S(2)}) copy-start(bf16[128,256]{1,0:T(8,128)(2,1)} %constant.57.clone.lh_ref) | copy-start | bytes 196612
  45.5 10.6 %copy-start.10 = (bf16[128,256]{1,0:T(8,128)(2,1)S(1)}, bf16[128,256]{1,0:T(8,128)(2,1)}, u32[]{:S(2)}) copy-start(bf16[128,256]{1,0:T(8,128)(2,1)} %constant.58.clone.ll_ref) | copy-start | bytes 196612
  56.1 34.1 %copy-start = (f32[64,1024]{1,0:T(8,128)S(1)}, f32[64,1024]{1,0:T(8,128)}, u32[]{:S(2)}) copy-start(f32[64,1024]{1,0:T(8,128)} %w_ref.1) | copy-start | bytes 786436
  56.1 34.1 %copy-start.1 = (s32[3,1024]{1,0:T(4,128)S(1)}, s32[3,1024]{1,0:T(4,128)}, u32[]{:S(2)}) copy-start(s32[3,1024]{1,0:T(4,128)} %cells_ref.1) | copy-start | bytes 36868
  56.1 34.1 %copy-start.11 = (bf16[128,128]{1,0:T(8,128)(2,1)S(1)}, bf16[128,128]{1,0:T(8,128)(2,1)}, u32[]{:S(2)}) copy-start(bf16[128,128]{1,0:T(8,128)(2,1)} %constant.59.clone.bh_ref) | copy-start | bytes 98308
  56.2 34.1 %copy-start.12 = (bf16[128,128]{1,0:T(8,128)(2,1)S(1)}, bf16[128,128]{1,0:T(8,128)(2,1)}, u32[]{:S(2)}) copy-start(bf16[128,128]{1,0:T(8,128)(2,1)} %constant.60.clone.bl_ref) | copy-start | bytes 98308

commit v3 on v2

--- a/solution.py
+++ b/solution.py
@@ -79,18 +79,18 @@
     m = np.repeat(np.arange(8), 4)
     n = np.tile(np.arange(4), 8)
     fine = turn(-(4 * m[None] * xl[:, None] + 8 * n[None] * yl[:, None]), 32) * used[:, None]
-    second = np.zeros((2, LANES, 2, 2, 32))
-    for ab in range(2):
-        second[0, :, ab, 0] = fine.real
-        second[1, :, ab, 0] = -fine.imag
-        second[0, :, ab, 1] = fine.imag
-        second[1, :, ab, 1] = fine.real
-    third = np.zeros((2, 2, 32, 2, 2, LANES))
-    for ab in range(2):
-        third[ab, 0, :, ab, 0] = fine.real.T
-        third[ab, 1, :, ab, 0] = fine.imag.T
-        third[ab, 0, :, ab, 1] = -fine.imag.T
-        third[ab, 1, :, ab, 1] = fine.real.T
+    second = np.zeros((2, LANES, 4, 2, 32))
+    second[0, :, :, 0] = fine.real[:, None]
+    second[1, :, :, 0] = -fine.imag[:, None]
+    second[0, :, :, 1] = fine.imag[:, None]
+    second[1, :, :, 1] = fine.real[:, None]
+    third = np.zeros((2, 32, 2, LANES))
+    third[0, :, 0] = fine.real.T
+    third[1, :, 0] = fine.imag.T
+    third[0, :, 1] = -fine.imag.T
+    third[1, :, 1] = fine.real.T
+    high, low = halves(third.reshape(64, 256))
+    third = np.concatenate([high, low, high, low])
     last = np.zeros((PZ, 2, 2, 2, PZ))
     last[:, 0, 0, 0] = wave.real.T
     last[:, 0, 0, 1] = wave.imag.T
@@ -98,7 +98,7 @@
     last[:, 1, 1, 1] = wave.real.T
     last = np.kron(np.eye(2), last.reshape(64, 128))
     twist = np.stack([twist.real, twist.imag]).astype(np.float32)
-    return first, twist, second.reshape(256, 128), third.reshape(128, 512), last
+    return first, twist, second.reshape(256, 256), third, last
 
 
 def split(value):
@@ -221,13 +221,15 @@
         )
 
 
-def plane_kernel(in_ref, filt_ref, fh_ref, fl_ref, tw_ref, sh_ref, sl_ref, th_ref, tl_ref, lh_ref, ll_ref, out_ref):
+def plane_kernel(in_ref, filt_ref, fh_ref, fl_ref, tw_ref, sh_ref, sl_ref, third_ref, lh_ref, ll_ref, out_ref):
     rows = []
-    for p4 in range(PY // 4):
-        high, low = split(in_ref[256 * p4 : 256 * (p4 + 1), :])
+    for p8 in range(PY // 8):
+        pair = jnp.concatenate([in_ref[512 * p8 : 512 * p8 + 256, :], in_ref[512 * p8 + 256 : 512 * p8 + 512, :]], axis=1)
+        high, low = split(pair)
         part = mm(fh_ref[...], high) + mm(fl_ref[...], high) + mm(fh_ref[...], low)
-        for p in range(4):
-            rows.append((part[64 * p : 64 * p + 32], part[64 * p + 32 : 64 * p + 64]))
+        for half in (part[:, :LANES], part[:, LANES:]):
+            for p in range(4):
+                rows.append((half[64 * p : 64 * p + 32], half[64 * p + 32 : 64 * p + 64]))
     rows = fft16(rows, -1)
     turned = []
     for k in range(PY):
@@ -235,35 +237,44 @@
         tr, ti = tw_ref[0, at, :], tw_ref[1, at, :]
         re, im = rows[k]
         turned.append(jnp.concatenate([re * tr - im * ti, im * tr + re * ti], axis=1))
-    high, low = split(jnp.concatenate(turned, axis=0))
-    spec = mm(high, sh_ref[...]) + mm(high, sl_ref[...]) + mm(low, sh_ref[...])
-    high, low = split(spec * filt_ref[...])
-    both = mm(high, th_ref[...]) + mm(high, tl_ref[...]) + mm(low, th_ref[...])
     back = []
-    for k in range(PY):
-        at = slice(PZ * k, PZ * (k + 1))
-        tr, ti = tw_ref[0, at, :], tw_ref[1, at, :]
-        cols = []
+    step = 8
+    for g in range(0, PY, step):
+        at = slice(PZ * g, PZ * (g + step))
+        high, low = split(jnp.concatenate(turned[g : g + step], axis=0))
+        spec = mm(high, sh_ref[...]) + mm(high, sl_ref[...]) + mm(low, sh_ref[...])
+        sides = []
         for ab in range(2):
-            re, im = both[at, 256 * ab : 256 * ab + 128], both[at, 256 * ab + 128 : 256 * ab + 256]
-            cols.append((re * tr + im * ti, im * tr - re * ti))
-        back.append(cols)
+            high, low = split(spec[:, 128 * ab : 128 * ab + 128] * filt_ref[at, 128 * ab : 128 * ab + 128])
+            sides.append(mm(jnp.concatenate([high, low], axis=1), third_ref[...]))
+        for k in range(step):
+            here = slice(PZ * k, PZ * (k + 1))
+            tr, ti = tw_ref[0, PZ * (g + k) : PZ * (g + k + 1), :], tw_ref[1, PZ * (g + k) : PZ * (g + k + 1), :]
+            cols = []
+            for side in sides:
+                re, im = side[here, :LANES], side[here, LANES:]
+                cols.append((re * tr + im * ti, im * tr - re * ti))
+            back.append(cols)
     a = fft16([cols[0] for cols in back], 1)
     b = fft16([cols[1] for cols in back], 1)
-    for p in range(0, PY, 2):
-        stack = jnp.concatenate([a[p][0], a[p][1], b[p][0], b[p][1], a[p + 1][0], a[p + 1][1], b[p + 1][0], b[p + 1][1]], axis=0)
-        high, low = split(stack)
-        out_ref[64 * p : 64 * (p + 2), :] = mm(lh_ref[...], high) + mm(ll_ref[...], high) + mm(lh_ref[...], low)
-
-
-def gather_kernel(in_ref, w_ref, cells_ref, bh_ref, bl_ref, out_ref, pot_ref, hit_ref, near_ref):
+    for p in range(0, PY, 4):
+        stack = []
+        for o in (p, p + 2):
+            stack.append(jnp.concatenate([a[o][0], a[o][1], b[o][0], b[o][1], a[o + 1][0], a[o + 1][1], b[o + 1][0], b[o + 1][1]], axis=0))
+        high, low = split(jnp.concatenate(stack, axis=1))
+        part = mm(lh_ref[...], high) + mm(ll_ref[...], high) + mm(lh_ref[...], low)
+        out_ref[64 * p : 64 * (p + 2), :] = part[:, :LANES]
+        out_ref[64 * (p + 2) : 64 * (p + 4), :] = part[:, LANES:]
+
+
+def gather_kernel(in_ref, w_ref, cells_ref, b_ref, out_ref, pot_ref, hit_ref):
     atoms = out_ref.shape[1]
     for c in range(0, CH, 2):
         pots = []
         for h in range(2):
             high, low = split(in_ref[(c + h) * 128 : (c + h + 1) * 128, :].T)
-            pot = mm(high, bh_ref[...]) + mm(high, bl_ref[...]) + mm(low, bh_ref[...])
-            pots.append(pot[:ROWS])
+            pot = mm(jnp.concatenate([high, low], axis=1), b_ref[...])
+            pots.append(pot[:ROWS, :MESH] + pot[:ROWS, MESH:])
         high, low = split(jnp.concatenate(pots, axis=0))
         pot_ref[c * ROWS : (c + 2) * ROWS, 0:MESH] = high
         pot_ref[c * ROWS : (c + 2) * ROWS, MESH : 2 * MESH] = low
@@ -275,14 +286,17 @@
             hit = z_hits(cells_ref, lo, k)
             hit_ref[slot, 0:MESH, k * TILE : (k + 1) * TILE] = hit
             hit_ref[slot, MESH : 2 * MESH, k * TILE : (k + 1) * TILE] = hit
-        near_ref[slot] = mm(pot_ref[...], hit_ref[slot])
-        for c in range(CH):
-            total = jnp.zeros((8, TILE), F32)
-            for x in range(EX):
-                for k in range(4):
-                    r = c * ROWS + 8 * x
-                    total = total + spread[x][k] * near_ref[slot, r : r + 8, k * TILE : (k + 1) * TILE]
-            out_ref[c : c + 1, lo : lo + TILE] = jnp.sum(total, axis=0, keepdims=True)
+        for c in range(0, CH, 2):
+            near = mm(pot_ref[c * ROWS : (c + 2) * ROWS, :], hit_ref[slot])
+            for h in range(2):
+                sums = [None] * 4
+                for x in range(EX):
+                    for k in range(4):
+                        r = h * ROWS + 8 * x
+                        term = spread[x][k] * near[r : r + 8, k * TILE : (k + 1) * TILE]
+                        sums[k] = term if x == 0 else sums[k] + term
+                total = (sums[0] + sums[1]) + (sums[2] + sums[3])
+                out_ref[c + h : c + h + 1, lo : lo + TILE] = jnp.sum(total, axis=0, keepdims=True)
 
 
 def call(kernel, out_shape, scratch, flops, moved, *args, space=pltpu.VMEM, limit=40):
@@ -313,19 +327,20 @@
     first, twist, second, third, last = plane_tables()
     return call(
         plane_kernel, (PY * PZ * 2, LANES), [], 10**9, 2 * 10**6,
-        blocks, filt, *halves(first), twist, *halves(second), *halves(third), *halves(last),
+        blocks, filt, *halves(first), twist, *halves(second), third, *halves(last),
     )
 
 
 def gather(blocks, spline_weights, base_cells):
     _, back = z_tables()
     atoms = spline_weights.shape[1]
+    high, low = halves(back)
+    table = np.block([[high, low], [high, low]])
     scratch = [
         pltpu.VMEM((CH * ROWS, 2 * MESH), BF16),
         pltpu.VMEM((2, 2 * MESH, 4 * TILE), BF16),
-        pltpu.VMEM((2, CH * ROWS, 4 * TILE), F32),
     ]
-    return call(gather_kernel, (CH, atoms), scratch, 3 * 10**9, 10**6, blocks, spline_weights, base_cells, *halves(back))
+    return call(gather_kernel, (CH, atoms), scratch, 3 * 10**9, 10**6, blocks, spline_weights, base_cells, table)
 
 
 def plane_filter(spectral_filter):
@@ -337,7 +352,7 @@
     shared = (q == half) & (p % 2 == 0)
     both = jnp.stack([jnp.where(shared, even, mine), mine], axis=1)
     both = both.reshape(4, 4, 2, 8, 8, 16).transpose(5, 1, 3, 2, 4, 0).reshape(PY * PZ, 2, 1, 32)
-    return jnp.broadcast_to(both, (PY * PZ, 2, 2, 32)).reshape(PY * PZ, 128)
+    return jnp.broadcast_to(both, (PY * PZ, 2, 4, 32)).reshape(PY * PZ, 256)
 
 
 def exchange(blocks):

time: 93.5 us -> 92.6 us (level)
  Pallas kernels: 11.6 us -> 10.6 us
    pallas_call x3, Pallas kernels: 11.6 us -> 10.6 us  [call(): pl.pallas_call(kernel, out_shape=jax.ShapeDtypeStruct(out_shape, F32), in...]
where the time goes in v3:
time: 92.6 us; the launch traced here: 92.2 us
  starting transfers between devices  35 us (38%)
  blocking collectives  31.4 us (34%)
  Pallas kernels  10.6 us (11%)
  waiting for transfers between devices  8.29 us (9%)
  local copies, waits for them, and re-layouts  6.64 us (7%)
    all_to_all x1, blocking collectives, exchange(): lax.all_to_all(blocks.reshape(PY * PZ, 2, LANES), ('py', 'pz'), 0, 0)  31.4 us
    all_to_all x1, starting transfers between devices, exchange(): lax.all_to_all(blocks.reshape(PY * PZ, 2, LANES), ('py', 'pz'), 0, 0)  17.5 us
    pallas_call x3, Pallas kernels, call(): pl.pallas_call(kernel, out_shape=jax.ShapeDtypeStruct(out_shape, F32), in...  10.6 us
    all_to_all x1, starting transfers between devices, plane_filter(): pair = lax.all_to_all(spectral_filter.reshape(PY, 2, BX, MESH), 'py', 0, 0)  10.2 us
    ppermute x1, starting transfers between devices, plane_filter(): even = lax.ppermute(pair[:, 0], 'pz', [(0, half)])  7.32 us
    all_to_all x1, waiting for transfers between devices, exchange(): lax.all_to_all(blocks.reshape(PY * PZ, 2, LANES), ('py', 'pz'), 0, 0)  6.23 us
    broadcast_in_dim x2, local copies, waits for them, and re-layouts, plane_filter(): return jnp.broadcast_to(both, (PY * PZ, 2, 4, 32)).reshape(PY * PZ, 256)  4.18 us
  transfers between devices with their start and end apart: 3, of which 3 were waited for; matrix products, arithmetic and copies ran while one was open for 7% of the time, Pallas kernels for 6%

profile of v3, /device:TPU:1, one launch (start us, length us, event | category | flops | bytes accessed | tf_op | source)
XLA Modules:
  0.0 92.2 jit_solution(16307100970271388314)
XLA Ops:
  0.0 10.2 %all-to-all-start.1 = ((f32[16,2,8,128]{3,2,1,0:T(8,128)}), f32[16,2,8,128]{3,2,1,0:T(8,128)S(1)}, u32[]{:S(2)}, u32[]{:S(2)}) async-start(f32[16,2,8,128]{3,2,1,0:T(8,128)} %bitcast.25), calls=%async_computation.1 | async-start | bytes 262144 | tf_op jit(solution)/shard_map/all_to_all | solution.py:349
  10.2 5.9 %shard_map.136 = f32[1024,128]{1,0:T(8,128)} custom-call(f32[8,1024]{1,0:T(8,128)} %cot_in.1, f32[64,1024]{1,0:T(8,128)} %w_ref.1, s32[3,1024]{1,0:T(4,128)} %cells_ref.1, bf16[2,128,128]{2,1,0:T(8,128)(2,1)} %constant.45.clone.m_in), custom_call_target="tpu_custom_call" | custom-call | flops 3000000000 | bytes 1000000 | tf_op jit(solution)/shard_map/pallas_call | solution.py:303
  16.1 0.3 all-to-all-done.1
  16.4 17.5 %all-to-all-start = ((f32[512,2,128]{2,1,0:T(2,128)}), f32[512,2,128]{2,1,0:T(2,128)S(1)}, u32[]{:S(2)}, u32[]{:S(2)}) async-start(f32[512,2,128]{2,1,0:T(2,128)} %bitcast.24), calls=%async_computation | async-start | bytes 1048576 | tf_op jit(solution)/shard_map/all_to_all | solution.py:359
  33.9 7.3 %collective-permute-start = (f32[16,8,128]{2,1,0:T(8,128)S(1)}, f32[16,8,128]{2,1,0:T(8,128)S(1)}, u32[]{:S(2)}, u32[]{:S(2)}) collective-permute-start(f32[16,8,128]{2,1,0:T(8,128)S(1)} %get-tuple-element.5), channel_id=1, source_target_pairs={{0,16},{32,48},{64,80},{96,112},{128,144},{160,176},{192,208},{224... | collective-permute-start | bytes 196616 | tf_op jit(solution)/shard_map/ppermute | solution.py:350
  41.2 0.2 stack.10
  41.4 1.8 %collective-permute-done = f32[16,8,128]{2,1,0:T(8,128)S(1)} collective-permute-done((f32[16,8,128]{2,1,0:T(8,128)S(1)}, f32[16,8,128]{2,1,0:T(8,128)S(1)}, u32[]{:S(2)}, u32[]{:S(2)}) %collective-permute-start) | collective-permute-done | bytes 65568 | tf_op jit(solution)/shard_map/ppermute | solution.py:350
  43.2 0.2 stack.9
  43.4 0.1 maximum_bitcast_fusion
  43.5 1.8 %copy.20 = f32[16,4,8,2,8,4]{2,1,0,5,4,3:T(4,128)} copy(f32[16,4,8,2,8,4]{0,4,2,1,5,3:T(8,128)S(1)} %maximum_bitcast_fusion) | data formatting | bytes 262144 | tf_op jit(solution)/shard_map/transpose | solution.py:354
  45.4 0.0 copy-start.2
  45.4 0.0 copy-start.4
  45.4 0.0 copy-start.5
  45.4 0.0 copy-start.6
  45.4 0.0 copy-start.7
  45.4 0.0 copy-start.8
  45.4 0.0 copy-start.9
  45.4 0.0 copy-start.10
  45.4 4.1 %broadcast_in_dim.7 = f32[512,2,32]{0,2,1:T(8,128)S(1)} reshape(f32[16,4,8,2,8,4]{2,1,0,5,4,3:T(4,128)} %copy.20) | data formatting | bytes 262144 | tf_op jit(solution)/shard_map/broadcast_in_dim | solution.py:355
  49.6 0.1 broadcast_in_dim.8
  49.6 0.2 copy.21.filt_ref
  49.8 6.2 %all-to-all-done = f32[512,2,128]{2,1,0:T(2,128)S(1)} async-done(((f32[512,2,128]{2,1,0:T(2,128)}), f32[512,2,128]{2,1,0:T(2,128)S(1)}, u32[]{:S(2)}, u32[]{:S(2)}) %all-to-all-start) | async-done | bytes 524320 | tf_op jit(solution)/shard_map/all_to_all | solution.py:359
  56.1 0.0 copy-done.2
  56.1 0.0 copy-done.4
  56.1 0.0 copy-done.5
  56.1 0.0 copy-done.6
  56.1 0.0 copy-done.7
  56.1 0.0 copy-done.8
  56.1 0.0 copy-done.9
  56.1 0.0 copy-done.10
  56.1 0.0 copy-start
  56.1 0.0 copy-start.1
  56.2 0.0 copy-start.3
  56.2 1.9 %shard_map.137 = f32[1024,128]{1,0:T(8,128)S(1)} custom-call(f32[1024,128]{1,0:T(8,128)S(1)} %bitcast.20, f32[512,256]{1,0:T(8,128)S(1)} %copy.21.filt_ref, bf16[256,256]{1,0:T(8,128)(2,1)S(1)} %copy-done.4, bf16[256,256]{1,0:T(8,128)(2,1)S(1)} %copy-done.5, f32[2,512,128]{2,1,0:T(8,128)S(1)} %copy-done.2, bf16[256,256]{1,0:T(8,128)(2,1)S(1)} %copy-done.6, ...), custom_call_target="tpu_custom_call" | custom-call | flops 1000000000 | bytes 2000000 | tf_op jit(solution)/shard_map/pallas_call | solution.py:303
  58.0 31.4 %all_to_all.15 = f32[512,2,128]{2,1,0:T(2,128)S(1)} all-to-all(f32[512,2,128]{2,1,0:T(2,128)S(1)} %bitcast.21), channel_id=1, replica_groups=mesh['py'=16,'pz'=32] {'py','pz'}, dimensions={0} | all-to-all | bytes 1048576 | tf_op jit(solution)/shard_map/all_to_all | solution.py:359
  89.4 0.0 copy-done
  89.4 0.0 copy-done.1
  89.4 0.0 copy-done.3
  89.4 2.8 %shard_map.138 = f32[8,1024]{1,0:T(8,128)} custom-call(f32[1024,128]{1,0:T(8,128)S(1)} %bitcast.22, f32[64,1024]{1,0:T(8,128)S(1)} %copy-done, s32[3,1024]{1,0:T(4,128)S(1)} %copy-done.1, bf16[256,256]{1,0:T(8,128)(2,1)S(1)} %copy-done.3), custom_call_target="tpu_custom_call" | custom-call | flops 3000000000 | bytes 1000000 | tf_op jit(solution)/shard_map/pallas_call | solution.py:303
  (2 shorter events, 0.0 us)
Async XLA Ops:
  0.0 16.4 %all-to-all-start.1 = ((f32[16,2,8,128]{3,2,1,0:T(8,128)}), f32[16,2,8,128]{3,2,1,0:T(8,128)S(1)}, u32[]{:S(2)}, u32[]{:S(2)}) async-start(f32[16,2,8,128]{3,2,1,0:T(8,128)} %bitcast.25), calls=%async_computation.1 | async-start | bytes 262144 | tf_op jit(solution)/shard_map/all_to_all | solution.py:349
  16.4 39.7 %all-to-all-start = ((f32[512,2,128]{2,1,0:T(2,128)}), f32[512,2,128]{2,1,0:T(2,128)S(1)}, u32[]{:S(2)}, u32[]{:S(2)}) async-start(f32[512,2,128]{2,1,0:T(2,128)} %bitcast.24), calls=%async_computation | async-start | bytes 1048576 | tf_op jit(solution)/shard_map/all_to_all | solution.py:359
  33.9 9.3 %collective-permute-start = (f32[16,8,128]{2,1,0:T(8,128)S(1)}, f32[16,8,128]{2,1,0:T(8,128)S(1)}, u32[]{:S(2)}, u32[]{:S(2)}) collective-permute-start(f32[16,8,128]{2,1,0:T(8,128)S(1)} %get-tuple-element.5), channel_id=1, source_target_pairs={{0,16},{32,48},{64,80},{96,112},{128,144},{160,176},{192,208},{224... | collective-permute-start | bytes 196616 | tf_op jit(solution)/shard_map/ppermute | solution.py:350
  45.4 10.7 %copy-start.2 = (f32[2,512,128]{2,1,0:T(8,128)S(1)}, f32[2,512,128]{2,1,0:T(8,128)}, u32[]{:S(2)}) copy-start(f32[2,512,128]{2,1,0:T(8,128)} %constant.48.clone.tw_ref) | copy-start | bytes 1572868
  45.4 10.7 %copy-start.4 = (bf16[256,256]{1,0:T(8,128)(2,1)S(1)}, bf16[256,256]{1,0:T(8,128)(2,1)}, u32[]{:S(2)}) copy-start(bf16[256,256]{1,0:T(8,128)(2,1)} %constant.46.clone.fh_ref) | copy-start | bytes 393220
  45.4 10.7 %copy-start.5 = (bf16[256,256]{1,0:T(8,128)(2,1)S(1)}, bf16[256,256]{1,0:T(8,128)(2,1)}, u32[]{:S(2)}) copy-start(bf16[256,256]{1,0:T(8,128)(2,1)} %constant.47.clone.fl_ref) | copy-start | bytes 393220
  45.4 10.7 %copy-start.6 = (bf16[256,256]{1,0:T(8,128)(2,1)S(1)}, bf16[256,256]{1,0:T(8,128)(2,1)}, u32[]{:S(2)}) copy-start(bf16[256,256]{1,0:T(8,128)(2,1)} %constant.49.clone.sh_ref) | copy-start | bytes 393220
  45.4 10.7 %copy-start.7 = (bf16[256,256]{1,0:T(8,128)(2,1)S(1)}, bf16[256,256]{1,0:T(8,128)(2,1)}, u32[]{:S(2)}) copy-start(bf16[256,256]{1,0:T(8,128)(2,1)} %constant.50.clone.sl_ref) | copy-start | bytes 393220
  45.4 10.7 %copy-start.8 = (bf16[256,256]{1,0:T(8,128)(2,1)S(1)}, bf16[256,256]{1,0:T(8,128)(2,1)}, u32[]{:S(2)}) copy-start(bf16[256,256]{1,0:T(8,128)(2,1)} %constant.51.clone.third_ref) | copy-start | bytes 393220
  45.4 10.7 %copy-start.9 = (bf16[128,256]{1,0:T(8,128)(2,1)S(1)}, bf16[128,256]{1,0:T(8,128)(2,1)}, u32[]{:S(2)}) copy-start(bf16[128,256]{1,0:T(8,128)(2,1)} %constant.52.clone.lh_ref) | copy-start | bytes 196612
  45.4 10.7 %copy-start.10 = (bf16[128,256]{1,0:T(8,128)(2,1)S(1)}, bf16[128,256]{1,0:T(8,128)(2,1)}, u32[]{:S(2)}) copy-start(bf16[128,256]{1,0:T(8,128)(2,1)} %constant.53.clone.ll_ref) | copy-start | bytes 196612
  56.1 33.3 %copy-start = (f32[64,1024]{1,0:T(8,128)S(1)}, f32[64,1024]{1,0:T(8,128)}, u32[]{:S(2)}) copy-start(f32[64,1024]{1,0:T(8,128)} %w_ref.1) | copy-start | bytes 786436
  56.1 33.3 %copy-start.1 = (s32[3,1024]{1,0:T(4,128)S(1)}, s32[3,1024]{1,0:T(4,128)}, u32[]{:S(2)}) copy-start(s32[3,1024]{1,0:T(4,128)} %cells_ref.1) | copy-start | bytes 36868
  56.2 33.2 %copy-start.3 = (bf16[256,256]{1,0:T(8,128)(2,1)S(1)}, bf16[256,256]{1,0:T(8,128)(2,1)}, u32[]{:S(2)}) copy-start(bf16[256,256]{1,0:T(8,128)(2,1)} %constant.54.clone.b_ref) | copy-start | bytes 393220

commit v4 on v3

--- a/solution.py
+++ b/solution.py
@@ -196,16 +196,19 @@
         for k in range(4):
             hit_ref[slot, k * TILE : (k + 1) * TILE, :] = jnp.where(zz == ((bz + k) & (MESH - 1)), 1.0, 0.0).astype(BF16)
         hit = hit_ref[slot]
-        for c in range(0, CH, 2):
-            cots = [jnp.broadcast_to(cot_ref[c + h : c + h + 1, lo : lo + TILE], (8, TILE)) for h in range(2)]
+        group = 4
+        for c in range(0, CH, group):
+            cots = [jnp.broadcast_to(cot_ref[c + h : c + h + 1, lo : lo + TILE], (8, TILE)) for h in range(group)]
             hs, ls = [], []
             for k in range(4):
-                g = jnp.concatenate([spread[x][k] * cots[h] for h in range(2) for x in range(EX)], axis=0)
+                g = jnp.concatenate([spread[x][k] * cots[h] for h in range(group) for x in range(EX)], axis=0)
                 high, low = split(g)
                 hs.append(high)
                 ls.append(low)
-            part = mm(jnp.concatenate(hs, axis=1), hit) + mm(jnp.concatenate(ls, axis=1), hit)
-            at = slice(c * ROWS, (c + 2) * ROWS)
+            both = jnp.concatenate([jnp.concatenate(hs, axis=1), jnp.concatenate(ls, axis=1)], axis=0)
+            part = mm(both, hit)
+            part = part[: group * ROWS] + part[group * ROWS :]
+            at = slice(c * ROWS, (c + group) * ROWS)
             if t == 0:
                 den_ref[at, :] = part
             else:
@@ -286,9 +289,9 @@
             hit = z_hits(cells_ref, lo, k)
             hit_ref[slot, 0:MESH, k * TILE : (k + 1) * TILE] = hit
             hit_ref[slot, MESH : 2 * MESH, k * TILE : (k + 1) * TILE] = hit
-        for c in range(0, CH, 2):
-            near = mm(pot_ref[c * ROWS : (c + 2) * ROWS, :], hit_ref[slot])
-            for h in range(2):
+        for c in range(0, CH, 4):
+            near = mm(pot_ref[c * ROWS : (c + 4) * ROWS, :], hit_ref[slot])
+            for h in range(4):
                 sums = [None] * 4
                 for x in range(EX):
                     for k in range(4):
@@ -343,16 +346,50 @@
     return call(gather_kernel, (CH, atoms), scratch, 3 * 10**9, 10**6, blocks, spline_weights, base_cells, table)
 
 
+def filter_kernel(flag_ref, pair_ref, even_ref, pick_ref, out_ref):
+    mine, other = [], []
+    for p in range(PY):
+        row = jnp.where(flag_ref[0] > 0, pair_ref[p, 1], pair_ref[p, 0])
+        mine.append(row)
+        other.append(jnp.where(flag_ref[1] > 0, even_ref[p], row))
+    lane = lax.broadcasted_iota(jnp.int32, (PZ, LANES), 1) & 3
+    for ab, rows in enumerate((other, mine)):
+        rest = jnp.concatenate(rows, axis=0)
+        parts = []
+        for _ in range(3):
+            part = rest.astype(BF16)
+            rest = rest - part.astype(F32)
+            parts.append(part)
+        wide = mm(jnp.concatenate(parts, axis=0), pick_ref[...])
+        wide = (wide[:MESH] + wide[MESH : 2 * MESH]) + wide[2 * MESH :]
+        for k in range(PY):
+            at = slice(LANES * k, LANES * (k + 1))
+            value = wide[0:PZ, at]
+            for n in range(1, 4):
+                value = jnp.where(lane == n, wide[PZ * n : PZ * (n + 1), at], value)
+            out_ref[PZ * k : PZ * (k + 1), LANES * ab : LANES * (ab + 1)] = value
+
+
 def plane_filter(spectral_filter):
     p, q = lax.axis_index("py"), lax.axis_index("pz")
     half = PZ // 2
     pair = lax.all_to_all(spectral_filter.reshape(PY, 2, BX, MESH), "py", 0, 0)
     even = lax.ppermute(pair[:, 0], "pz", [(0, half)])
-    mine = jnp.where(q < half, pair[:, 1], pair[:, 0])
-    shared = (q == half) & (p % 2 == 0)
-    both = jnp.stack([jnp.where(shared, even, mine), mine], axis=1)
-    both = both.reshape(4, 4, 2, 8, 8, 16).transpose(5, 1, 3, 2, 4, 0).reshape(PY * PZ, 2, 1, 32)
-    return jnp.broadcast_to(both, (PY * PZ, 2, 4, 32)).reshape(PY * PZ, 256)
+    flags = jnp.stack([q < half, (q == half) & (p % 2 == 0)]).astype(jnp.int32)
+    pick = np.zeros((8, PY, PY, 4, 8, 4))
+    for m in range(8):
+        for k in range(PY):
+            pick[m, k, k, :, m, :] = 1.0
+    pick = pick.reshape(MESH, PY * LANES).astype(ml_dtypes.bfloat16)
+    vmem = pl.BlockSpec(memory_space=pltpu.VMEM)
+    return pl.pallas_call(
+        filter_kernel,
+        out_shape=jax.ShapeDtypeStruct((PY * PZ, 2 * LANES), F32),
+        in_specs=[pl.BlockSpec(memory_space=pltpu.SMEM), vmem, vmem, vmem],
+        out_specs=vmem,
+        compiler_params=pltpu.CompilerParams(vmem_limit_bytes=32 * 1024 * 1024),
+        cost_estimate=pl.CostEstimate(flops=10**9, bytes_accessed=10**6, transcendentals=0),
+    )(flags, pair, even, pick)
 
 
 def exchange(blocks):

time: 92.6 us -> 91.7 us (level)
  local copies, waits for them, and re-layouts: 6.64 us -> 0.07 us
  waiting for transfers between devices: 8.29 us -> 13.8 us
  Pallas kernels: 10.6 us -> 11.7 us
    all_to_all x1, waiting for transfers between devices: 6.23 us -> 11.4 us  [exchange(): lax.all_to_all(blocks.reshape(PY * PZ, 2, LANES), ('py', 'pz'), 0, 0)]
    broadcast_in_dim x2 -> x0, local copies, waits for them, and re-layouts: 4.18 us -> none  [plane_filter(): return jnp.broadcast_to(both, (PY * PZ, 2, 4, 32)).reshape(PY * PZ, 256)]
    transpose x1 -> x0, local copies, waits for them, and re-layouts: 1.84 us -> none  [plane_filter(): both.reshape(4, 4, 2, 8, 8, 16).transpose(5, 1, 3, 2, 4, 0)]
    pallas_call x0 -> x1, Pallas kernels: none -> 1.49 us  [plane_filter(): pl.pallas_call(filter_kernel, out_shape=jax.ShapeDtypeStruct((PY * PZ, 2...]
  transfers between devices with their start and end apart: 3 -> 3, of which waited for: 3 -> 3; matrix products, arithmetic and copies ran while one was open for 7% -> 0% of each run, Pallas kernels for 6% -> 8%
where the time goes in v4:
time: 91.7 us; the launch traced here: 91.3 us
  starting transfers between devices  34.7 us (38%)
  blocking collectives  30.8 us (34%)
  waiting for transfers between devices  13.8 us (15%)
  Pallas kernels  11.7 us (13%)
    all_to_all x1, blocking collectives, exchange(): lax.all_to_all(blocks.reshape(PY * PZ, 2, LANES), ('py', 'pz'), 0, 0)  30.8 us
    all_to_all x1, starting transfers between devices, exchange(): lax.all_to_all(blocks.reshape(PY * PZ, 2, LANES), ('py', 'pz'), 0, 0)  17.2 us
    all_to_all x1, waiting for transfers between devices, exchange(): lax.all_to_all(blocks.reshape(PY * PZ, 2, LANES), ('py', 'pz'), 0, 0)  11.4 us
    pallas_call x3, Pallas kernels, call(): pl.pallas_call(kernel, out_shape=jax.ShapeDtypeStruct(out_shape, F32), in...  10.2 us
    all_to_all x1, starting transfers between devices, plane_filter(): pair = lax.all_to_all(spectral_filter.reshape(PY, 2, BX, MESH), 'py', 0, 0)  10.2 us
    ppermute x1, starting transfers between devices, plane_filter(): even = lax.ppermute(pair[:, 0], 'pz', [(0, half)])  7.32 us
    ppermute x1, waiting for transfers between devices, plane_filter(): even = lax.ppermute(pair[:, 0], 'pz', [(0, half)])  1.85 us
  transfers between devices with their start and end apart: 3, of which 3 were waited for; matrix products, arithmetic and copies ran while one was open for 0% of the time, Pallas kernels for 8%

profile of v4, /device:TPU:1, one launch (start us, length us, event | category | flops | bytes accessed | tf_op | source)
XLA Modules:
  0.0 91.3 jit_solution(6902043705313467330)
XLA Ops:
  0.0 10.2 %all-to-all-start.1 = ((f32[16,2,8,128]{3,2,1,0:T(8,128)}), f32[16,2,8,128]{3,2,1,0:T(8,128)S(1)}, u32[]{:S(2)}, u32[]{:S(2)}) async-start(f32[16,2,8,128]{3,2,1,0:T(8,128)} %bitcast.15), calls=%async_computation.1 | async-start | bytes 262144 | tf_op jit(solution)/shard_map/all_to_all | solution.py:376
  10.2 5.7 %shard_map.145 = f32[1024,128]{1,0:T(8,128)} custom-call(f32[8,1024]{1,0:T(8,128)} %cot_in.1, f32[64,1024]{1,0:T(8,128)} %w_ref.1, s32[3,1024]{1,0:T(4,128)} %cells_ref.1, bf16[2,128,128]{2,1,0:T(8,128)(2,1)} %constant.48.clone.m_in), custom_call_target="tpu_custom_call" | custom-call | flops 3000000000 | bytes 1000000 | tf_op jit(solution)/shard_map/pallas_call | solution.py:306
  15.8 0.6 all-to-all-done.1.pair_ref
  16.4 0.0 copy-start.3
  16.4 17.2 %all-to-all-start = ((f32[512,2,128]{2,1,0:T(2,128)}), f32[512,2,128]{2,1,0:T(2,128)S(1)}, u32[]{:S(2)}, u32[]{:S(2)}) async-start(f32[512,2,128]{2,1,0:T(2,128)} %bitcast.14), calls=%async_computation | async-start | bytes 1048576 | tf_op jit(solution)/shard_map/all_to_all | solution.py:396
  33.6 7.3 %collective-permute-start = (f32[16,8,128]{2,1,0:T(8,128)S(1)}, f32[16,8,128]{2,1,0:T(8,128)S(1)}, u32[]{:S(2)}, u32[]{:S(2)}) collective-permute-start(f32[16,8,128]{2,1,0:T(8,128)S(1)} %slice_bitcast_fusion), channel_id=1, source_target_pairs={{0,16},{32,48},{64,80},{96,112},{128,144},{160,176},{192,208},{224... | collective-permute-start | bytes 196616 | tf_op jit(solution)/shard_map/ppermute | solution.py:377
  41.0 0.1 add_convert_fusion.flag_ref
  41.0 0.0 copy-start.2
  41.0 0.0 copy-start.5
  41.0 0.0 copy-start.6
  41.0 0.0 copy-start.7
  41.0 0.0 copy-start.8
  41.1 0.0 copy-start.9
  41.1 0.0 copy-start.10
  41.1 0.0 copy-start.11
  41.1 1.9 %collective-permute-done.even_ref = f32[16,8,128]{2,1,0:T(8,128)S(1)} collective-permute-done((f32[16,8,128]{2,1,0:T(8,128)S(1)}, f32[16,8,128]{2,1,0:T(8,128)S(1)}, u32[]{:S(2)}, u32[]{:S(2)}) %collective-permute-start) | collective-permute-done | bytes 65568 | tf_op jit(solution)/shard_map/ppermute | solution.py:377
  42.9 0.0 copy-done.3
  43.0 1.5 %shard_map.146.filt_ref = f32[512,256]{1,0:T(8,128)S(1)} custom-call(s32[2]{0:T(128)S(1)} %add_convert_fusion.flag_ref, f32[16,2,8,128]{3,2,1,0:T(8,128)S(1)} %all-to-all-done.1.pair_ref, f32[16,8,128]{2,1,0:T(8,128)S(1)} %collective-permute-done.even_ref, bf16[128,2048]{1,0:T(8,128)(2,1)S(1)} %copy-done.3), custom_call_target="tpu_custom_call" | custom-call | flops 1000000000 | bytes 1000000 | tf_op jit(solution)/shard_map/pallas_call | solution.py:385
  44.5 11.4 %all-to-all-done = f32[512,2,128]{2,1,0:T(2,128)S(1)} async-done(((f32[512,2,128]{2,1,0:T(2,128)}), f32[512,2,128]{2,1,0:T(2,128)S(1)}, u32[]{:S(2)}, u32[]{:S(2)}) %all-to-all-start) | async-done | bytes 524320 | tf_op jit(solution)/shard_map/all_to_all | solution.py:396
  55.8 0.0 copy-done.2
  55.8 0.0 copy-done.5
  55.8 0.0 copy-done.6
  55.8 0.0 copy-done.7
  55.8 0.0 copy-done.8
  55.8 0.0 copy-done.9
  55.8 0.0 copy-done.10
  55.9 0.0 copy-done.11
  55.9 1.9 %shard_map.147 = f32[1024,128]{1,0:T(8,128)S(1)} custom-call(f32[1024,128]{1,0:T(8,128)S(1)} %bitcast.11, f32[512,256]{1,0:T(8,128)S(1)} %shard_map.146.filt_ref, bf16[256,256]{1,0:T(8,128)(2,1)S(1)} %copy-done.5, bf16[256,256]{1,0:T(8,128)(2,1)S(1)} %copy-done.6, f32[2,512,128]{2,1,0:T(8,128)S(1)} %copy-done.2, bf16[256,256]{1,0:T(8,128)(2,1)S(1)} %copy-done.7, ...), custom_call_target="tpu_custom_call" | custom-call | flops 1000000000 | bytes 2000000 | tf_op jit(solution)/shard_map/pallas_call | solution.py:306
  57.7 0.0 copy-start
  57.7 0.0 copy-start.1
  57.7 0.0 copy-start.4
  57.8 30.8 %all_to_all.15 = f32[512,2,128]{2,1,0:T(2,128)S(1)} all-to-all(f32[512,2,128]{2,1,0:T(2,128)S(1)} %bitcast.12), channel_id=1, replica_groups=mesh['py'=16,'pz'=32] {'py','pz'}, dimensions={0} | all-to-all | bytes 1048576 | tf_op jit(solution)/shard_map/all_to_all | solution.py:396
  88.6 0.0 copy-done
  88.6 0.0 copy-done.1
  88.6 0.0 copy-done.4
  88.6 2.7 %shard_map.148 = f32[8,1024]{1,0:T(8,128)} custom-call(f32[1024,128]{1,0:T(8,128)S(1)} %bitcast.13, f32[64,1024]{1,0:T(8,128)S(1)} %copy-done, s32[3,1024]{1,0:T(4,128)S(1)} %copy-done.1, bf16[256,256]{1,0:T(8,128)(2,1)S(1)} %copy-done.4), custom_call_target="tpu_custom_call" | custom-call | flops 3000000000 | bytes 1000000 | tf_op jit(solution)/shard_map/pallas_call | solution.py:306
  (1 shorter events, 0.0 us)
Async XLA Ops:
  0.0 16.4 %all-to-all-start.1 = ((f32[16,2,8,128]{3,2,1,0:T(8,128)}), f32[16,2,8,128]{3,2,1,0:T(8,128)S(1)}, u32[]{:S(2)}, u32[]{:S(2)}) async-start(f32[16,2,8,128]{3,2,1,0:T(8,128)} %bitcast.15), calls=%async_computation.1 | async-start | bytes 262144 | tf_op jit(solution)/shard_map/all_to_all | solution.py:376
  16.4 26.5 %copy-start.3 = (bf16[128,2048]{1,0:T(8,128)(2,1)S(1)}, bf16[128,2048]{1,0:T(8,128)(2,1)}, u32[]{:S(2)}) copy-start(bf16[128,2048]{1,0:T(8,128)(2,1)} %constant.47.clone.pick_ref) | copy-start | bytes 1572868
  16.4 39.4 %all-to-all-start = ((f32[512,2,128]{2,1,0:T(2,128)}), f32[512,2,128]{2,1,0:T(2,128)S(1)}, u32[]{:S(2)}, u32[]{:S(2)}) async-start(f32[512,2,128]{2,1,0:T(2,128)} %bitcast.14), calls=%async_computation | async-start | bytes 1048576 | tf_op jit(solution)/shard_map/all_to_all | solution.py:396
  33.6 9.3 %collective-permute-start = (f32[16,8,128]{2,1,0:T(8,128)S(1)}, f32[16,8,128]{2,1,0:T(8,128)S(1)}, u32[]{:S(2)}, u32[]{:S(2)}) collective-permute-start(f32[16,8,128]{2,1,0:T(8,128)S(1)} %slice_bitcast_fusion), channel_id=1, source_target_pairs={{0,16},{32,48},{64,80},{96,112},{128,144},{160,176},{192,208},{224... | collective-permute-start | bytes 196616 | tf_op jit(solution)/shard_map/ppermute | solution.py:377
  41.0 14.8 %copy-start.2 = (f32[2,512,128]{2,1,0:T(8,128)S(1)}, f32[2,512,128]{2,1,0:T(8,128)}, u32[]{:S(2)}) copy-start(f32[2,512,128]{2,1,0:T(8,128)} %constant.51.clone.tw_ref) | copy-start | bytes 1572868
  41.0 14.8 %copy-start.5 = (bf16[256,256]{1,0:T(8,128)(2,1)S(1)}, bf16[256,256]{1,0:T(8,128)(2,1)}, u32[]{:S(2)}) copy-start(bf16[256,256]{1,0:T(8,128)(2,1)} %constant.49.clone.fh_ref) | copy-start | bytes 393220
  41.0 14.8 %copy-start.6 = (bf16[256,256]{1,0:T(8,128)(2,1)S(1)}, bf16[256,256]{1,0:T(8,128)(2,1)}, u32[]{:S(2)}) copy-start(bf16[256,256]{1,0:T(8,128)(2,1)} %constant.50.clone.fl_ref) | copy-start | bytes 393220
  41.0 14.8 %copy-start.7 = (bf16[256,256]{1,0:T(8,128)(2,1)S(1)}, bf16[256,256]{1,0:T(8,128)(2,1)}, u32[]{:S(2)}) copy-start(bf16[256,256]{1,0:T(8,128)(2,1)} %constant.52.clone.sh_ref) | copy-start | bytes 393220
  41.0 14.8 %copy-start.8 = (bf16[256,256]{1,0:T(8,128)(2,1)S(1)}, bf16[256,256]{1,0:T(8,128)(2,1)}, u32[]{:S(2)}) copy-start(bf16[256,256]{1,0:T(8,128)(2,1)} %constant.53.clone.sl_ref) | copy-start | bytes 393220
  41.1 14.8 %copy-start.9 = (bf16[256,256]{1,0:T(8,128)(2,1)S(1)}, bf16[256,256]{1,0:T(8,128)(2,1)}, u32[]{:S(2)}) copy-start(bf16[256,256]{1,0:T(8,128)(2,1)} %constant.54.clone.third_ref) | copy-start | bytes 393220
  41.1 14.8 %copy-start.10 = (bf16[128,256]{1,0:T(8,128)(2,1)S(1)}, bf16[128,256]{1,0:T(8,128)(2,1)}, u32[]{:S(2)}) copy-start(bf16[128,256]{1,0:T(8,128)(2,1)} %constant.55.clone.lh_ref) | copy-start | bytes 196612
  41.1 14.8 %copy-start.11 = (bf16[128,256]{1,0:T(8,128)(2,1)S(1)}, bf16[128,256]{1,0:T(8,128)(2,1)}, u32[]{:S(2)}) copy-start(bf16[128,256]{1,0:T(8,128)(2,1)} %constant.56.clone.ll_ref) | copy-start | bytes 196612
  57.7 30.9 %copy-start = (f32[64,1024]{1,0:T(8,128)S(1)}, f32[64,1024]{1,0:T(8,128)}, u32[]{:S(2)}) copy-start(f32[64,1024]{1,0:T(8,128)} %w_ref.1) | copy-start | bytes 786436
  57.7 30.9 %copy-start.1 = (s32[3,1024]{1,0:T(4,128)S(1)}, s32[3,1024]{1,0:T(4,128)}, u32[]{:S(2)}) copy-start(s32[3,1024]{1,0:T(4,128)} %cells_ref.1) | copy-start | bytes 36868
  57.7 30.9 %copy-start.4 = (bf16[256,256]{1,0:T(8,128)(2,1)S(1)}, bf16[256,256]{1,0:T(8,128)(2,1)}, u32[]{:S(2)}) copy-start(bf16[256,256]{1,0:T(8,128)(2,1)} %constant.57.clone.b_ref) | copy-start | bytes 393220

commit v5 on v4

--- a/solution.py
+++ b/solution.py
@@ -18,6 +18,8 @@
 EX = BX + 3
 ROWS = EX * 8
 LANES = 128
+OWN = BX * 8
+EDGE = 3 * 8
 TILE = 128
 
 F32 = jnp.float32
@@ -53,7 +55,7 @@
     forth[0, PZ // 2, 1] = sign
     back[0, PZ // 2, 0] = scale
     back[0, PZ // 2, 1] = scale * sign
-    return forth.reshape(128, MESH), back.reshape(128, MESH)
+    return forth.reshape(128, MESH), back.reshape(64, 2 * MESH)
 
 
 def plane_tables():
@@ -84,6 +86,7 @@
     second[1, :, :, 0] = -fine.imag[:, None]
     second[0, :, :, 1] = fine.imag[:, None]
     second[1, :, :, 1] = fine.real[:, None]
+    fine = np.where(np.arange(LANES)[:, None] < OWN, fine, 0.0)
     third = np.zeros((2, 32, 2, LANES))
     third[0, :, 0] = fine.real.T
     third[1, :, 0] = fine.imag.T
@@ -91,11 +94,11 @@
     third[1, :, 1] = fine.real.T
     high, low = halves(third.reshape(64, 256))
     third = np.concatenate([high, low, high, low])
-    last = np.zeros((PZ, 2, 2, 2, PZ))
-    last[:, 0, 0, 0] = wave.real.T
-    last[:, 0, 0, 1] = wave.imag.T
-    last[:, 1, 1, 0] = -wave.imag.T
-    last[:, 1, 1, 1] = wave.real.T
+    last = np.zeros((2, PZ, 2, 2, PZ))
+    last[0, :, 0, 0] = wave.real.T
+    last[0, :, 0, 1] = wave.imag.T
+    last[1, :, 1, 0] = -wave.imag.T
+    last[1, :, 1, 1] = wave.real.T
     last = np.kron(np.eye(2), last.reshape(64, 128))
     twist = np.stack([twist.real, twist.imag]).astype(np.float32)
     return first, twist, second.reshape(256, 256), third, last
@@ -145,7 +148,7 @@
     return out
 
 
-def atom_weights(w_ref, cells_ref, lo):
+def atom_weights(w_ref, cells_ref, lo, layers):
     at = slice(lo, lo + TILE)
     lx = cells_ref[0:1, at] & (BX - 1)
     ly = cells_ref[1:2, at] & (BY - 1)
@@ -162,14 +165,16 @@
                 row = jnp.broadcast_to(w_ref[16 * i + 4 * j + k : 16 * i + 4 * j + k + 1, at], (8, TILE))
                 value = jnp.where(on_y[j], row, value)
             rows[i][k] = value
-    spread = [[None] * 4 for _ in range(EX)]
-    for x in range(EX):
+    spread = []
+    for x in layers:
+        values = []
         for k in range(4):
             value = zero
             for i in range(4):
                 if 0 <= x - i < BX:
                     value = jnp.where(on_x[x - i], rows[i][k], value)
-            spread[x][k] = value
+            values.append(value)
+        spread.append(values)
     return spread
 
 
@@ -190,7 +195,7 @@
     for t in range(atoms // TILE):
         lo = t * TILE
         slot = t % 2
-        spread = atom_weights(w_ref, cells_ref, lo)
+        spread = atom_weights(w_ref, cells_ref, lo, range(EX))
         bz = jnp.broadcast_to(cells_ref[2:3, lo : lo + TILE], (TILE, TILE)).T
         zz = lax.broadcasted_iota(jnp.int32, (TILE, MESH), 1)
         for k in range(4):
@@ -266,52 +271,76 @@
             stack.append(jnp.concatenate([a[o][0], a[o][1], b[o][0], b[o][1], a[o + 1][0], a[o + 1][1], b[o + 1][0], b[o + 1][1]], axis=0))
         high, low = split(jnp.concatenate(stack, axis=1))
         part = mm(lh_ref[...], high) + mm(ll_ref[...], high) + mm(lh_ref[...], low)
-        out_ref[64 * p : 64 * (p + 2), :] = part[:, :LANES]
-        out_ref[64 * (p + 2) : 64 * (p + 4), :] = part[:, LANES:]
-
-
-def gather_kernel(in_ref, w_ref, cells_ref, b_ref, out_ref, pot_ref, hit_ref):
-    atoms = out_ref.shape[1]
+        for o in range(4):
+            at, lane = 64 * (o % 2), LANES * (o // 2)
+            re, im = part[at : at + PZ, lane : lane + LANES], part[at + PZ : at + 64, lane : lane + LANES]
+            out_ref[PZ * (p + o) : PZ * (p + o + 1), :] = re + pltpu.roll(im, OWN, 1)
+
+
+def potential_kernel(in_ref, bh_ref, bl_ref, own_ref, edge_ref):
     for c in range(0, CH, 2):
         pots = []
         for h in range(2):
-            high, low = split(in_ref[(c + h) * 128 : (c + h + 1) * 128, :].T)
-            pot = mm(jnp.concatenate([high, low], axis=1), b_ref[...])
-            pots.append(pot[:ROWS, :MESH] + pot[:ROWS, MESH:])
+            high, low = split(in_ref[(c + h) * 64 : (c + h + 1) * 64, :].T)
+            pot = mm(high, bh_ref[...]) + mm(high, bl_ref[...]) + mm(low, bh_ref[...])
+            pot = pot[:OWN, :MESH] + pot[OWN:, MESH:]
+            edge_ref[(c + h) * EDGE : (c + h + 1) * EDGE, :] = pot[:EDGE]
+            pots.append(pot)
         high, low = split(jnp.concatenate(pots, axis=0))
-        pot_ref[c * ROWS : (c + 2) * ROWS, 0:MESH] = high
-        pot_ref[c * ROWS : (c + 2) * ROWS, MESH : 2 * MESH] = low
-    for t in range(atoms // TILE):
+        own_ref[c * OWN : (c + 2) * OWN, 0:MESH] = high
+        own_ref[c * OWN : (c + 2) * OWN, MESH : 2 * MESH] = low
+
+
+def read_back(pot_ref, w_ref, cells_ref, hit_ref, out_ref, layers, before):
+    count = 8 * len(layers)
+    group = 4 if count > 32 else CH
+    for t in range(out_ref.shape[1] // TILE):
         lo = t * TILE
         slot = t % 2
-        spread = atom_weights(w_ref, cells_ref, lo)
+        spread = atom_weights(w_ref, cells_ref, lo, layers)
         for k in range(4):
             hit = z_hits(cells_ref, lo, k)
             hit_ref[slot, 0:MESH, k * TILE : (k + 1) * TILE] = hit
             hit_ref[slot, MESH : 2 * MESH, k * TILE : (k + 1) * TILE] = hit
-        for c in range(0, CH, 4):
-            near = mm(pot_ref[c * ROWS : (c + 4) * ROWS, :], hit_ref[slot])
-            for h in range(4):
+        for c in range(0, CH, group):
+            near = mm(pot_ref[c * count : (c + group) * count, :], hit_ref[slot])
+            for h in range(group):
                 sums = [None] * 4
-                for x in range(EX):
+                for x, row in enumerate(spread):
                     for k in range(4):
-                        r = h * ROWS + 8 * x
-                        term = spread[x][k] * near[r : r + 8, k * TILE : (k + 1) * TILE]
+                        r = h * count + 8 * x
+                        term = row[k] * near[r : r + 8, k * TILE : (k + 1) * TILE]
                         sums[k] = term if x == 0 else sums[k] + term
-                total = (sums[0] + sums[1]) + (sums[2] + sums[3])
-                out_ref[c + h : c + h + 1, lo : lo + TILE] = jnp.sum(total, axis=0, keepdims=True)
-
-
-def call(kernel, out_shape, scratch, flops, moved, *args, space=pltpu.VMEM, limit=40):
-    return pl.pallas_call(
+                total = jnp.sum((sums[0] + sums[1]) + (sums[2] + sums[3]), axis=0, keepdims=True)
+                if before is not None:
+                    total = total + before[c + h : c + h + 1, lo : lo + TILE]
+                out_ref[c + h : c + h + 1, lo : lo + TILE] = total
+
+
+def own_kernel(pot_ref, w_ref, cells_ref, out_ref, hit_ref):
+    read_back(pot_ref, w_ref, cells_ref, hit_ref, out_ref, range(BX), None)
+
+
+def gather_kernel(edge_ref, before_ref, w_ref, cells_ref, out_ref, pot_ref, hit_ref):
+    high, low = split(edge_ref[...])
+    pot_ref[:, 0:MESH] = high
+    pot_ref[:, MESH : 2 * MESH] = low
+    read_back(pot_ref, w_ref, cells_ref, hit_ref, out_ref, range(BX, EX), before_ref)
+
+
+def call(kernel, outs, scratch, flops, moved, *args, space=pltpu.VMEM, limit=40):
+    shapes = [jax.ShapeDtypeStruct(*out) for out in outs]
+    specs = [pl.BlockSpec(memory_space=pltpu.VMEM) for _ in outs]
+    result = pl.pallas_call(
         kernel,
-        out_shape=jax.ShapeDtypeStruct(out_shape, F32),
+        out_shape=shapes,
         in_specs=[pl.BlockSpec(memory_space=space)] * len(args),
-        out_specs=pl.BlockSpec(memory_space=pltpu.VMEM),
+        out_specs=specs,
         scratch_shapes=scratch,
         compiler_params=pltpu.CompilerParams(vmem_limit_bytes=limit * 1024 * 1024),
         cost_estimate=pl.CostEstimate(flops=flops, bytes_accessed=moved, transcendentals=0),
     )(*args)
+    return result[0] if len(outs) == 1 else result
 
 
 def scatter(cotangent, spline_weights, base_cells):
@@ -323,27 +352,35 @@
         pltpu.VMEM((CH * ROWS, MESH), F32),
         pltpu.SemaphoreType.DMA((4,)),
     ]
-    return call(scatter_kernel, (CH * 128, LANES), scratch, 3 * 10**9, 10**6, *args, space=pltpu.HBM, limit=60)
+    return call(scatter_kernel, [((CH * 128, LANES), F32)], scratch, 3 * 10**9, 10**6, *args, space=pltpu.HBM, limit=60)
 
 
 def plane(blocks, filt):
     first, twist, second, third, last = plane_tables()
     return call(
-        plane_kernel, (PY * PZ * 2, LANES), [], 10**9, 2 * 10**6,
+        plane_kernel, [((PY * PZ, LANES), F32)], [], 10**9, 2 * 10**6,
         blocks, filt, *halves(first), twist, *halves(second), third, *halves(last),
     )
 
 
-def gather(blocks, spline_weights, base_cells):
+def potential(blocks):
     _, back = z_tables()
-    atoms = spline_weights.shape[1]
-    high, low = halves(back)
-    table = np.block([[high, low], [high, low]])
-    scratch = [
-        pltpu.VMEM((CH * ROWS, 2 * MESH), BF16),
-        pltpu.VMEM((2, 2 * MESH, 4 * TILE), BF16),
-    ]
-    return call(gather_kernel, (CH, atoms), scratch, 3 * 10**9, 10**6, blocks, spline_weights, base_cells, table)
+    outs = [((CH * OWN, 2 * MESH), BF16), ((CH * EDGE, MESH), F32)]
+    return call(potential_kernel, outs, [], 10**9, 10**6, blocks, *halves(back))
+
+
+def hits():
+    return pltpu.VMEM((2, 2 * MESH, 4 * TILE), BF16)
+
+
+def gather_own(own, spline_weights, base_cells):
+    outs = [((CH, spline_weights.shape[1]), F32)]
+    return call(own_kernel, outs, [hits()], 3 * 10**9, 10**6, own, spline_weights, base_cells)
+
+
+def gather(edge, before, spline_weights, base_cells):
+    scratch = [pltpu.VMEM((CH * EDGE, 2 * MESH), BF16), hits()]
+    return call(gather_kernel, [(before.shape, F32)], scratch, 10**9, 10**6, edge, before, spline_weights, base_cells)
 
 
 def filter_kernel(flag_ref, pair_ref, even_ref, pick_ref, out_ref):
@@ -393,7 +430,8 @@
 
 
 def exchange(blocks):
-    return lax.all_to_all(blocks.reshape(PY * PZ, 2, LANES), ("py", "pz"), 0, 0).reshape(PY * PZ * 2, LANES)
+    rows = blocks.shape[0] // (PY * PZ)
+    return lax.all_to_all(blocks.reshape(PY * PZ, rows, LANES), ("py", "pz"), 0, 0).reshape(blocks.shape)
 
 
 def on_device(cotangent, spline_weights, base_cells, spectral_filter):
@@ -402,7 +440,10 @@
     blocks = exchange(blocks)
     blocks = plane(blocks, filt)
     blocks = exchange(blocks)
-    return gather(blocks, spline_weights, base_cells)
+    own, edge = potential(blocks)
+    edge = lax.ppermute(edge, "py", [(p, (p - 1) % PY) for p in range(PY)])
+    before = gather_own(own, spline_weights, base_cells)
+    return gather(edge, before, spline_weights, base_cells)
 
 
 def solution(mesh):

time: 91.7 us -> 92.2 us (level)
  blocking collectives: 30.8 us -> 25.9 us
  waiting for transfers between devices: 13.8 us -> 16.3 us
  starting transfers between devices: 34.7 us -> 36.6 us
  Pallas kernels: 11.7 us -> 12.7 us
    all_to_all x1, blocking collectives: 30.8 us -> 25.9 us  [exchange(): lax.all_to_all(blocks.reshape(PY * PZ, rows, LANES), ('py', 'pz'), 0, 0)]
    ppermute x0 -> x1, waiting for transfers between devices: none -> 2.58 us  [on_device(): edge = lax.ppermute(edge, 'py', [(p, (p - 1) % PY) for p in range(PY)])]
    ppermute x0 -> x1, starting transfers between devices: none -> 1.92 us  [on_device(): edge = lax.ppermute(edge, 'py', [(p, (p - 1) % PY) for p in range(PY)])]
    pallas_call x3 -> x5, Pallas kernels: 10.2 us -> 11.2 us  [call(): pl.pallas_call(kernel, out_shape=shapes, in_specs=[pl.BlockSpec(memory_sp...]
  transfers between devices with their start and end apart: 3 -> 4, of which waited for: 3 -> 4; matrix products, arithmetic and copies ran while one was open for 0% -> 0% of each run, Pallas kernels for 8% -> 9%
where the time goes in v5:
time: 92.2 us; the launch traced here: 91.9 us
  starting transfers between devices  36.6 us (40%)
  blocking collectives  25.9 us (28%)
  waiting for transfers between devices  16.3 us (18%)
  Pallas kernels  12.7 us (14%)
    all_to_all x1, blocking collectives, exchange(): lax.all_to_all(blocks.reshape(PY * PZ, rows, LANES), ('py', 'pz'), 0, 0)  25.9 us
    all_to_all x1, starting transfers between devices, exchange(): lax.all_to_all(blocks.reshape(PY * PZ, rows, LANES), ('py', 'pz'), 0, 0)  17.2 us
    all_to_all x1, waiting for transfers between devices, exchange(): lax.all_to_all(blocks.reshape(PY * PZ, rows, LANES), ('py', 'pz'), 0, 0)  11.3 us
    pallas_call x5, Pallas kernels, call(): pl.pallas_call(kernel, out_shape=shapes, in_specs=[pl.BlockSpec(memory_sp...  11.2 us
    all_to_all x1, starting transfers between devices, plane_filter(): pair = lax.all_to_all(spectral_filter.reshape(PY, 2, BX, MESH), 'py', 0, 0)  10.2 us
    ppermute x1, starting transfers between devices, plane_filter(): even = lax.ppermute(pair[:, 0], 'pz', [(0, half)])  7.32 us
    ppermute x1, waiting for transfers between devices, on_device(): edge = lax.ppermute(edge, 'py', [(p, (p - 1) % PY) for p in range(PY)])  2.58 us
    ppermute x1, starting transfers between devices, on_device(): edge = lax.ppermute(edge, 'py', [(p, (p - 1) % PY) for p in range(PY)])  1.92 us
  transfers between devices with their start and end apart: 4, of which 4 were waited for; matrix products, arithmetic and copies ran while one was open for 0% of the time, Pallas kernels for 9%

profile of v5, /device:TPU:1, one launch (start us, length us, event | category | flops | bytes accessed | tf_op | source)
XLA Modules:
  0.0 91.9 jit_solution(3396083018176295780)
XLA Ops:
  0.0 10.2 %all-to-all-start.1 = ((f32[16,2,8,128]{3,2,1,0:T(8,128)}), f32[16,2,8,128]{3,2,1,0:T(8,128)S(1)}, u32[]{:S(2)}, u32[]{:S(2)}) async-start(f32[16,2,8,128]{3,2,1,0:T(8,128)} %bitcast.17), calls=%async_computation.1 | async-start | bytes 262144 | tf_op jit(solution)/shard_map/all_to_all | solution.py:413
  10.2 5.7 %shard_map.154 = f32[1024,128]{1,0:T(8,128)} custom-call(f32[8,1024]{1,0:T(8,128)} %cot_in.1, f32[64,1024]{1,0:T(8,128)} %w_ref.3, s32[3,1024]{1,0:T(4,128)} %cells_ref.3, bf16[2,128,128]{2,1,0:T(8,128)(2,1)} %constant.50.clone.m_in), custom_call_target="tpu_custom_call" | custom-call | flops 3000000000 | bytes 1000000 | tf_op jit(solution)/shard_map/pallas_call | solution.py:334
  15.9 0.6 all-to-all-done.1.pair_ref
  16.4 0.0 copy-start.3
  16.4 17.2 %all-to-all-start = ((f32[512,2,128]{2,1,0:T(2,128)}), f32[512,2,128]{2,1,0:T(2,128)S(1)}, u32[]{:S(2)}, u32[]{:S(2)}) async-start(f32[512,2,128]{2,1,0:T(2,128)} %bitcast.16), calls=%async_computation | async-start | bytes 1048576 | tf_op jit(solution)/shard_map/all_to_all | solution.py:434
  33.6 7.3 %collective-permute-start = (f32[16,8,128]{2,1,0:T(8,128)S(1)}, f32[16,8,128]{2,1,0:T(8,128)S(1)}, u32[]{:S(2)}, u32[]{:S(2)}) collective-permute-start(f32[16,8,128]{2,1,0:T(8,128)S(1)} %slice_bitcast_fusion), channel_id=1, source_target_pairs={{0,16},{32,48},{64,80},{96,112},{128,144},{160,176},{192,208},{224... | collective-permute-start | bytes 196616 | tf_op jit(solution)/shard_map/ppermute | solution.py:414
  41.0 0.1 add_convert_fusion.flag_ref
  41.0 0.0 copy-start.2
  41.0 0.0 copy-start.4
  41.0 0.0 copy-start.5
  41.0 0.0 copy-start.6
  41.0 0.0 copy-start.7
  41.1 0.0 copy-start.8
  41.1 0.0 copy-start.9
  41.1 0.0 copy-start.10
  41.1 1.9 %collective-permute-done.even_ref = f32[16,8,128]{2,1,0:T(8,128)S(1)} collective-permute-done((f32[16,8,128]{2,1,0:T(8,128)S(1)}, f32[16,8,128]{2,1,0:T(8,128)S(1)}, u32[]{:S(2)}, u32[]{:S(2)}) %collective-permute-start) | collective-permute-done | bytes 65568 | tf_op jit(solution)/shard_map/ppermute | solution.py:414
  43.0 0.0 copy-done.3
  43.0 1.5 %shard_map.155.filt_ref = f32[512,256]{1,0:T(8,128)S(1)} custom-call(s32[2]{0:T(128)S(1)} %add_convert_fusion.flag_ref, f32[16,2,8,128]{3,2,1,0:T(8,128)S(1)} %all-to-all-done.1.pair_ref, f32[16,8,128]{2,1,0:T(8,128)S(1)} %collective-permute-done.even_ref, bf16[128,2048]{1,0:T(8,128)(2,1)S(1)} %copy-done.3), custom_call_target="tpu_custom_call" | custom-call | flops 1000000000 | bytes 1000000 | tf_op jit(solution)/shard_map/pallas_call | solution.py:422
  44.5 11.3 %all-to-all-done = f32[512,2,128]{2,1,0:T(2,128)S(1)} async-done(((f32[512,2,128]{2,1,0:T(2,128)}), f32[512,2,128]{2,1,0:T(2,128)S(1)}, u32[]{:S(2)}, u32[]{:S(2)}) %all-to-all-start) | async-done | bytes 524320 | tf_op jit(solution)/shard_map/all_to_all | solution.py:434
  55.8 0.0 copy-done.2
  55.8 0.0 copy-done.4
  55.8 0.0 copy-done.5
  55.8 0.0 copy-done.6
  55.8 0.0 copy-done.7
  55.8 0.0 copy-done.8
  55.8 0.0 copy-done.9
  55.8 0.0 copy-done.10
  55.8 1.9 %shard_map.156 = f32[512,128]{1,0:T(8,128)S(1)} custom-call(f32[1024,128]{1,0:T(8,128)S(1)} %bitcast.13, f32[512,256]{1,0:T(8,128)S(1)} %shard_map.155.filt_ref, bf16[256,256]{1,0:T(8,128)(2,1)S(1)} %copy-done.4, bf16[256,256]{1,0:T(8,128)(2,1)S(1)} %copy-done.5, f32[2,512,128]{2,1,0:T(8,128)S(1)} %copy-done.2, bf16[256,256]{1,0:T(8,128)(2,1)S(1)} %copy-done.6, ...), custom_call_target="tpu_custom_call" | custom-call | flops 1000000000 | bytes 2000000 | tf_op jit(solution)/shard_map/pallas_call | solution.py:334
  57.8 0.0 copy-start.11
  57.8 0.0 copy-start.12
  57.8 25.9 %all_to_all.15 = f32[512,1,128]{2,1,0:T(1,128)S(1)} all-to-all(f32[512,1,128]{2,1,0:T(1,128)S(1)} %bitcast.14), channel_id=1, replica_groups=mesh['py'=16,'pz'=32] {'py','pz'}, dimensions={0} | all-to-all | bytes 524288 | tf_op jit(solution)/shard_map/all_to_all | solution.py:434
  83.7 0.0 copy-done.11
  83.7 0.0 copy-done.12
  83.7 0.0 copy-start
  83.7 0.0 copy-start.1
  83.7 0.6 shard_map.157
  84.3 1.9 %collective-permute-start.1 = (f32[192,128]{1,0:T(8,128)S(1)}, f32[192,128]{1,0:T(8,128)S(1)}, u32[]{:S(2)}, u32[]{:S(2)}) collective-permute-start(f32[192,128]{1,0:T(8,128)S(1)} %get-tuple-element.7), channel_id=1, source_target_pairs={{0,480},{32,0},{64,32},{96,64},{128,96},{160,128},{192,160},{224,1... | collective-permute-start | bytes 294920 | tf_op jit(solution)/shard_map/ppermute | solution.py:444
  86.2 0.0 copy-done
  86.2 0.0 copy-done.1
  86.3 1.4 %shard_map.158.before_ref = f32[8,1024]{1,0:T(8,128)S(1)} custom-call(bf16[512,256]{1,0:T(8,128)(2,1)S(1)} %get-tuple-element.8.pot_ref, f32[64,1024]{1,0:T(8,128)S(1)} %copy-done, s32[3,1024]{1,0:T(4,128)S(1)} %copy-done.1), custom_call_target="tpu_custom_call" | custom-call | flops 3000000000 | bytes 1000000 | tf_op jit(solution)/shard_map/pallas_call | solution.py:334
  87.7 2.6 %collective-permute-done.1.edge_ref = f32[192,128]{1,0:T(8,128)S(1)} collective-permute-done((f32[192,128]{1,0:T(8,128)S(1)}, f32[192,128]{1,0:T(8,128)S(1)}, u32[]{:S(2)}, u32[]{:S(2)}) %collective-permute-start.1) | collective-permute-done | bytes 98336 | tf_op jit(solution)/shard_map/ppermute | solution.py:444
  90.2 1.6 %shard_map.159 = f32[8,1024]{1,0:T(8,128)} custom-call(f32[192,128]{1,0:T(8,128)S(1)} %collective-permute-done.1.edge_ref, f32[8,1024]{1,0:T(8,128)S(1)} %shard_map.158.before_ref, f32[64,1024]{1,0:T(8,128)S(1)} %copy-done, s32[3,1024]{1,0:T(4,128)S(1)} %copy-done.1), custom_call_target="tpu_custom_call" | custom-call | flops 1000000000 | bytes 1000000 | tf_op jit(solution)/shard_map/pallas_call | solution.py:334
  (1 shorter events, 0.0 us)
Async XLA Ops:
  0.0 16.4 %all-to-all-start.1 = ((f32[16,2,8,128]{3,2,1,0:T(8,128)}), f32[16,2,8,128]{3,2,1,0:T(8,128)S(1)}, u32[]{:S(2)}, u32[]{:S(2)}) async-start(f32[16,2,8,128]{3,2,1,0:T(8,128)} %bitcast.17), calls=%async_computation.1 | async-start | bytes 262144 | tf_op jit(solution)/shard_map/all_to_all | solution.py:413
  16.4 26.5 %copy-start.3 = (bf16[128,2048]{1,0:T(8,128)(2,1)S(1)}, bf16[128,2048]{1,0:T(8,128)(2,1)}, u32[]{:S(2)}) copy-start(bf16[128,2048]{1,0:T(8,128)(2,1)} %constant.49.clone.pick_ref) | copy-start | bytes 1572868
  16.4 39.4 %all-to-all-start = ((f32[512,2,128]{2,1,0:T(2,128)}), f32[512,2,128]{2,1,0:T(2,128)S(1)}, u32[]{:S(2)}, u32[]{:S(2)}) async-start(f32[512,2,128]{2,1,0:T(2,128)} %bitcast.16), calls=%async_computation | async-start | bytes 1048576 | tf_op jit(solution)/shard_map/all_to_all | solution.py:434
  33.6 9.3 %collective-permute-start = (f32[16,8,128]{2,1,0:T(8,128)S(1)}, f32[16,8,128]{2,1,0:T(8,128)S(1)}, u32[]{:S(2)}, u32[]{:S(2)}) collective-permute-start(f32[16,8,128]{2,1,0:T(8,128)S(1)} %slice_bitcast_fusion), channel_id=1, source_target_pairs={{0,16},{32,48},{64,80},{96,112},{128,144},{160,176},{192,208},{224... | collective-permute-start | bytes 196616 | tf_op jit(solution)/shard_map/ppermute | solution.py:414
  41.0 14.7 %copy-start.2 = (f32[2,512,128]{2,1,0:T(8,128)S(1)}, f32[2,512,128]{2,1,0:T(8,128)}, u32[]{:S(2)}) copy-start(f32[2,512,128]{2,1,0:T(8,128)} %constant.53.clone.tw_ref) | copy-start | bytes 1572868
  41.0 14.7 %copy-start.4 = (bf16[256,256]{1,0:T(8,128)(2,1)S(1)}, bf16[256,256]{1,0:T(8,128)(2,1)}, u32[]{:S(2)}) copy-start(bf16[256,256]{1,0:T(8,128)(2,1)} %constant.51.clone.fh_ref) | copy-start | bytes 393220
  41.0 14.7 %copy-start.5 = (bf16[256,256]{1,0:T(8,128)(2,1)S(1)}, bf16[256,256]{1,0:T(8,128)(2,1)}, u32[]{:S(2)}) copy-start(bf16[256,256]{1,0:T(8,128)(2,1)} %constant.52.clone.fl_ref) | copy-start | bytes 393220
  41.0 14.7 %copy-start.6 = (bf16[256,256]{1,0:T(8,128)(2,1)S(1)}, bf16[256,256]{1,0:T(8,128)(2,1)}, u32[]{:S(2)}) copy-start(bf16[256,256]{1,0:T(8,128)(2,1)} %constant.54.clone.sh_ref) | copy-start | bytes 393220
  41.0 14.7 %copy-start.7 = (bf16[256,256]{1,0:T(8,128)(2,1)S(1)}, bf16[256,256]{1,0:T(8,128)(2,1)}, u32[]{:S(2)}) copy-start(bf16[256,256]{1,0:T(8,128)(2,1)} %constant.55.clone.sl_ref) | copy-start | bytes 393220
  41.1 14.7 %copy-start.8 = (bf16[256,256]{1,0:T(8,128)(2,1)S(1)}, bf16[256,256]{1,0:T(8,128)(2,1)}, u32[]{:S(2)}) copy-start(bf16[256,256]{1,0:T(8,128)(2,1)} %constant.56.clone.third_ref) | copy-start | bytes 393220
  41.1 14.7 %copy-start.9 = (bf16[128,256]{1,0:T(8,128)(2,1)S(1)}, bf16[128,256]{1,0:T(8,128)(2,1)}, u32[]{:S(2)}) copy-start(bf16[128,256]{1,0:T(8,128)(2,1)} %constant.57.clone.lh_ref) | copy-start | bytes 196612
  41.1 14.7 %copy-start.10 = (bf16[128,256]{1,0:T(8,128)(2,1)S(1)}, bf16[128,256]{1,0:T(8,128)(2,1)}, u32[]{:S(2)}) copy-start(bf16[128,256]{1,0:T(8,128)(2,1)} %constant.58.clone.ll_ref) | copy-start | bytes 196612
  57.8 25.9 %copy-start.11 = (bf16[64,256]{1,0:T(8,128)(2,1)S(1)}, bf16[64,256]{1,0:T(8,128)(2,1)}, u32[]{:S(2)}) copy-start(bf16[64,256]{1,0:T(8,128)(2,1)} %constant.59.clone.bh_ref) | copy-start | bytes 98308
  57.8 25.9 %copy-start.12 = (bf16[64,256]{1,0:T(8,128)(2,1)S(1)}, bf16[64,256]{1,0:T(8,128)(2,1)}, u32[]{:S(2)}) copy-start(bf16[64,256]{1,0:T(8,128)(2,1)} %constant.60.clone.bl_ref) | copy-start | bytes 98308
  83.7 2.6 %copy-start = (f32[64,1024]{1,0:T(8,128)S(1)}, f32[64,1024]{1,0:T(8,128)}, u32[]{:S(2)}) copy-start(f32[64,1024]{1,0:T(8,128)} %w_ref.3) | copy-start | bytes 786436
  83.7 2.6 %copy-start.1 = (s32[3,1024]{1,0:T(4,128)S(1)}, s32[3,1024]{1,0:T(4,128)}, u32[]{:S(2)}) copy-start(s32[3,1024]{1,0:T(4,128)} %cells_ref.3) | copy-start | bytes 36868
  84.3 5.9 %collective-permute-start.1 = (f32[192,128]{1,0:T(8,128)S(1)}, f32[192,128]{1,0:T(8,128)S(1)}, u32[]{:S(2)}, u32[]{:S(2)}) collective-permute-start(f32[192,128]{1,0:T(8,128)S(1)} %get-tuple-element.7), channel_id=1, source_target_pairs={{0,480},{32,0},{64,32},{96,64},{128,96},{160,128},{192,160},{224,1... | collective-permute-start | bytes 294920 | tf_op jit(solution)/shard_map/ppermute | solution.py:444
